TPU v7x, 32 devices: a whole 2x2x4 slice. The times are simulated.
32 devices in a mesh: seq: 8 (over y, x, core), head: 4 (over z).
Axes of the slice: x: 2, y: 2, z: 4, core: 2. Of those that a mesh axis runs over, the one named last changes fastest.
Arguments:
- tokens: bfloat16 [16384, 2048], P(('seq', 'head')), may hold values from -6 to 6
- w_query: bfloat16 [2048, 2048], P(None, 'head'), may hold values from -0.125 to 0.125
- w_key: bfloat16 [2048, 2048], P(None, 'head'), may hold values from -0.125 to 0.125
- w_value: bfloat16 [2048, 2048], P(None, 'head'), may hold values from -0.125 to 0.125
- w_beta: bfloat16 [2048, 16], P(None, 'head'), may hold values from -0.125 to 0.125
- beta_gain: float32 [16], P('head'), may hold values from 0.0005 to 0.5
- norm_gain: float32 [2048], P('head'), may hold values from 0.1 to 1.9
- w_out: bfloat16 [2048, 2048], P('head'), may hold values from -0.125 to 0.125
Outputs:
- mixed: bfloat16 [16384, 2048], P(('seq', 'head'))
All inputs are finite; a program needn't handle non-finite values.
Results may differ from a plain program's by a relative error of at most 0.0085.
Values may be sent and summed in bfloat16 or wider, within the bound.
A program may use at most 192 MiB of HBM per device.

v0:
```python
import jax
import jax.numpy as jnp
from jax import lax
from jax.sharding import PartitionSpec as P

SPAN = 64


highest = lax.Precision.HIGHEST


def entering(part, axis, combine, identity):
    place = lax.axis_index(axis)
    gathered = jax.tree.map(lambda a: lax.all_gather(a, axis), part)
    state = jax.tree.map(lambda a, e: jnp.zeros_like(a) + jnp.asarray(e, a.dtype), part, identity)

    def one(turn, state):
        return combine(
            state, jax.tree.map(lambda a: lax.dynamic_index_in_dim(a, turn, 0, False), gathered)
        )

    return lax.fori_loop(0, place, one, state)


def mat(left, right):
    return jnp.einsum("...ij,...jk->...ik", left, right, precision=highest)


def mat_t(left, right):
    return jnp.einsum("...ji,...jk->...ik", left, right, precision=highest)


def gram_bt(left, right):
    return jnp.einsum("...ij,...kj->...ik", left, right, preferred_element_type=jnp.float32)


def unit_norm(raw):
    return raw / jnp.sqrt(jnp.sum(raw * raw, -1, keepdims=True) + 1e-06)


def span_terms(gram, keys, values, rates):
    size = keys.shape[-2]
    eye = jnp.eye(size, dtype=keys.dtype)
    lower = jnp.tril(rates[..., :, None] * gram, -1)
    inverse = eye - lower
    power = lower
    for level in range(size.bit_length() - 2):
        power = mat(power, power)
        inverse = mat(inverse, eye + power)
    weights = mat(inverse, rates[..., :, None] * keys)
    updates = mat(inverse, rates[..., :, None] * values)
    return (weights, updates)


def combine_pairs(earlier, later):
    first_m, first_b = earlier
    second_m, second_b = later
    return (mat(second_m, first_m), mat(second_m, first_b) + second_b)


def body(tokens, w_query, w_key, w_value, w_beta, beta_gain, norm_gain, w_out):
    per = w_query.shape[1]
    heads = w_beta.shape[1]
    width = per // heads
    piece = lax.all_gather(tokens, "head", axis=0, tiled=True)
    projected = jnp.concatenate(
        [
            jnp.dot(piece, w_query, preferred_element_type=jnp.float32),
            jnp.dot(piece, w_key, preferred_element_type=jnp.float32),
            jnp.dot(piece, w_value, preferred_element_type=jnp.float32),
            jnp.dot(piece, w_beta, preferred_element_type=jnp.float32),
        ],
        1,
    )
    rows = projected.shape[0]

    def stored(part):
        rounded = part.astype(jnp.bfloat16)
        return lax.optimization_barrier(rounded).astype(jnp.float32).reshape(rows, heads, width)

    query_half = unit_norm(stored(projected[:, :per])).astype(jnp.bfloat16)
    key_half = unit_norm(stored(projected[:, per : 2 * per])).astype(jnp.bfloat16)
    value = stored(projected[:, 2 * per : 3 * per])
    beta = beta_gain[None, :] * jax.nn.sigmoid(projected[:, 3 * per :])
    count = rows // SPAN

    def blocks(array):
        return array.reshape(count, SPAN, heads, width).transpose(0, 2, 1, 3)

    q_half_blocks = blocks(query_half)
    k_half_blocks = blocks(key_half)
    q_blocks = q_half_blocks.astype(jnp.float32)
    k_blocks = k_half_blocks.astype(jnp.float32)
    v_blocks = blocks(value)
    b_blocks = beta.reshape(count, SPAN, heads).transpose(0, 2, 1)
    key_gram = gram_bt(k_half_blocks, k_half_blocks)
    weights, updates = span_terms(key_gram, k_blocks, v_blocks, b_blocks)
    eye_state = jnp.broadcast_to(jnp.eye(width, dtype=jnp.float32), (heads, width, width))
    zero_state = jnp.zeros((heads, width, width), jnp.float32)

    def fold(carry, inputs):
        k_blk, w_blk, u_blk = inputs
        step_pair = (eye_state - mat_t(k_blk, w_blk), mat_t(k_blk, u_blk))
        return (combine_pairs(carry, step_pair), carry)

    (trans_dev, adds_dev), starts = lax.scan(
        fold, (eye_state, zero_state), (k_blocks, weights, updates), unroll=2
    )
    prefix = entering((trans_dev, adds_dev), "seq", combine_pairs, (eye_state, zero_state))
    incoming = prefix[1]
    causal = jnp.tril(jnp.ones((SPAN, SPAN), jnp.float32))

    def emit(state, inputs):
        q_blk, q_half, k_half, k_blk, w_blk, u_blk = inputs
        fresh = u_blk - mat(w_blk, state)
        out = mat(q_blk, state) + mat(causal * gram_bt(q_half, k_half), fresh)
        return (state + mat_t(k_blk, fresh), out)

    final, outs = lax.scan(
        emit,
        incoming,
        (q_blocks, q_half_blocks, k_half_blocks, k_blocks, weights, updates),
        unroll=2,
    )
    heads_out = outs.transpose(0, 2, 1, 3).reshape(rows, heads, width)
    scaled = heads_out / jnp.sqrt(jnp.mean(heads_out * heads_out, -1, keepdims=True) + 1e-05)
    normed = (scaled * norm_gain.reshape(heads, width)).reshape(rows, per).astype(jnp.bfloat16)
    piece = normed
    mixed = lax.psum_scatter(
        jnp.dot(piece, w_out, preferred_element_type=jnp.float32),
        "head",
        scatter_dimension=0,
        tiled=True,
    )
    return mixed.astype(jnp.bfloat16)


def solution(mesh):
    placed = (
        P(("seq", "head"), None),
        P(None, "head"),
        P(None, "head"),
        P(None, "head"),
        P(None, "head"),
        P("head"),
        P("head"),
        P("head", None),
    )
    return jax.shard_map(
        body, mesh=mesh, in_specs=placed, out_specs=P(("seq", "head"), None), check_vma=False
    )
```

profile of v0, /device:TPU:0, one launch (start us, length us, event | category | flops | bytes accessed | tf_op | source)
XLA Modules:
  0.0 978.2 jit_solution(10635402580201143054)
XLA Ops:
  7.4 153.9 %all-gather.6.cloned.1.call-done = bf16[2048,2048]{1,0:T(8,128)(2,1)} async-done(((bf16[512,2048]{1,0:T(8,128)(2,1)}), bf16[2048,2048]{1,0:T(8,128)(2,1)}) %all-gather.6.cloned.1.call-update) | async-done | bytes 8388624 | tf_op jit(solution)/shard_map/all_gather | solution.py:65
  161.3 8.5 convolution_convert_fusion.2
  171.1 2.6 convert_multiply_fusion.1
  173.7 5.0 reshape.139
  178.7 5.7 fusion.51
  184.5 9.8 %convolution_convert_fusion.1 = bf16[2048,512]{1,0:T(8,128)(2,1)} fusion(bf16[2048,2048]{1,0:T(8,128)(2,1)} %all-gather.6.cloned.1.call-done, bf16[2048,512]{1,0:T(8,128)(2,1)} %param.17), kind=kOutput, calls=%fused_computation.86 | convolution fusion | flops 4296015872 | bytes 12582912 | tf_op jit(solution)/shard_map/dot_general | solution.py:70
  194.3 4.8 reshape.150
  199.1 5.3 mul.72
  204.3 6.0 reduce_sum.27
  210.3 2.5 add_sqrt_fusion.1
  212.8 1.6 copy.31
  214.4 6.5 bitcast_convert_fusion
  222.2 5.3 fusion.47
  227.5 4.7 fusion.81
  232.2 5.4 fusion.44
  237.6 5.4 fusion.82
  243.0 5.0 fusion.42
  248.0 4.8 fusion.83
  252.8 5.2 fusion.40
  258.0 4.7 fusion.84
  262.7 5.4 fusion.38
  268.1 5.0 fusion.36
  273.1 5.9 fusion.34
  279.0 5.8 fusion.31
  284.8 127.1 %while.42 = (s32[]{:T(128)}, f32[4,128,128]{2,1,0:T(8,128)S(1)}, f32[4,128,128]{2,1,0:T(8,128)S(1)}, f32[16,2,4,64,128]{4,3,2,1,0:T(8,128)}, f32[16,2,4,64,128]{...) while((s32[]{:T(128)}, f32[4,128,128]{2,1,0:T(8,128)S(1)}, ...), condition=%wide.region_2.3_spmd.clone.clone, body=%wide.region_1.0_spmd.clone.clone.sunk | while | flops 604307456 | bytes 5904515 | solution.py:106
  285.0 1.6 convolution_subtract_fusion.10
  291.3 1.6 convolution_add_fusion.16
  299.3 1.6 convolution_add_fusion.16
  300.9 1.6 convolution_subtract_fusion.10
  307.2 1.6 convolution_add_fusion.16
  315.1 1.6 convolution_add_fusion.16
  316.7 1.6 convolution_subtract_fusion.10
  323.1 1.6 convolution_add_fusion.16
  324.7 1.6 convolution_subtract_fusion.10
  331.0 1.6 convolution_add_fusion.16
  332.6 1.6 convolution_subtract_fusion.10
  338.9 1.6 convolution_add_fusion.16
  340.5 1.6 convolution_subtract_fusion.10
  346.9 1.6 convolution_add_fusion.16
  354.8 1.6 convolution_add_fusion.16
  356.4 1.6 convolution_subtract_fusion.10
  362.7 1.6 convolution_add_fusion.16
  370.7 1.6 convolution_add_fusion.16
  372.3 1.6 convolution_subtract_fusion.10
  378.6 1.6 convolution_add_fusion.16
  386.5 1.6 convolution_add_fusion.16
  394.5 1.6 convolution_add_fusion.16
  402.4 1.6 convolution_add_fusion.16
  410.3 1.6 convolution_add_fusion.16
  413.4 9.8 %convolution_convert_fusion = bf16[2048,512]{1,0:T(8,128)(2,1)} fusion(bf16[2048,2048]{1,0:T(8,128)(2,1)} %all-gather.6.cloned.1.call-done, bf16[2048,512]{1,0:T(8,128)(2,1)} %param.15), kind=kOutput, calls=%fused_computation.85 | convolution fusion | flops 4296015872 | bytes 12582912 | tf_op jit(solution)/shard_map/dot_general | solution.py:68
  423.3 4.8 reshape.144
  428.0 4.2 convert_multiply_fusion
  432.2 5.3 mul.81
  437.5 5.1 reduce_sum.28
  442.8 4.4 fusion.68
  449.1 2.4 reshape.146
  451.6 17.2 %all-gather.8.cloned.1.call-done = f32[32,128,128]{2,1,0:T(8,128)} async-done(((f32[4,128,128]{2,1,0:T(8,128)}), f32[32,128,128]{2,1,0:T(8,128)}) %all-gather.8.cloned.1.call-update) | async-done | bytes 2097168 | tf_op jit(solution)/shard_map/all_gather | solution.py:14
  469.0 185.6 %while.41 = (s32[]{:T(128)}, f32[4,128,128]{2,1,0:T(8,128)S(1)}, f32[16,2,4,64,128]{4,3,2,1,0:T(8,128)}, f32[16,2,4,64,128]{4,3,2,1,0:T(8,128)}, f32[16,2,4,64,1...) while((s32[]{:T(128)}, f32[4,128,128]{2,1,0:T(8,128)S(1)}, ...), condition=%wide.region_7.8_spmd.clone.clone, body=%wide.region_6.7_spmd.clone.clone.sunk | while | flops 361078784 | bytes 5822629 | solution.py:119
  654.7 5.2 fusion.30
  659.9 3.6 copy.39
  663.9 4.7 div.45
  668.6 8.1 fusion.52
  676.7 290.7 %reduce-scatter.2.cloned.1.call-done = f32[512,2048]{1,0:T(8,128)} async-done(((f32[2048,2048]{1,0:T(8,128)}), f32[512,2048]{1,0:T(8,128)}) %reduce-scatter.2.cloned.1.call-update) | async-done | bytes 4194320 | tf_op jit(solution)/shard_map/reduce_scatter | solution.py:129
  967.4 3.8 convert_element_type.69
  (342 shorter events, 279.9 us)
Async XLA Ops:
  6.5 662.0 %copy-start = (bf16[512,2048]{1,0:T(8,128)(2,1)S(1)}, bf16[512,2048]{1,0:T(8,128)(2,1)}, u32[]{:S(2)}) copy-start(bf16[512,2048]{1,0:T(8,128)(2,1)} %param.21) | copy-start | bytes 6291460
  6.5 154.8 %all-gather.6.cloned.1.call-start = ((), (), s32[]{:S(2)}) async-start(), calls=%async_computation.1 | async-start | bytes 10485760 | tf_op jit(solution)/shard_map/all_gather | solution.py:65
  7.3 444.3 %all-gather.10.cloned.1.call-start = ((), (), s32[]{:S(2)}) async-start(), calls=%async_computation.4 | async-start | bytes 2359296 | tf_op jit(solution)/shard_map/all_gather | solution.py:14
  169.8 1.3 copy-start.7
  173.7 5.0 copy-start.8
  173.7 5.0 copy-start.9
  220.9 52.1 %copy-start.1 = (bf16[32,64,4,128]{3,1,2,0:T(8,128)(2,1)}, bf16[32,64,4,128]{3,1,2,0:T(8,128)(2,1)S(1)}, u32[]{:S(2)}) copy-start(bf16[32,64,4,128]{3,1,2,0:T(8,128)(2,1)S(1)} %get-tuple-element.281) | copy-start | bytes 6291460
  273.1 5.9 copy-start.2
  411.9 0.7 copy-start.6
  411.9 0.8 copy-start.4
  412.6 56.1 %all-gather.8.cloned.1.call-start = ((), (), s32[]{:S(2)}) async-start(), calls=%async_computation.3 | async-start | bytes 2359296 | tf_op jit(solution)/shard_map/all_gather | solution.py:14
  413.4 554.1 %reduce-scatter.2.cloned.1.call-start = ((), (), s32[]{:S(2)}) async-start(), calls=%async_computation.2 | async-start | bytes 20971520 | tf_op jit(solution)/shard_map/reduce_scatter | solution.py:129
  447.8 1.3 copy-start.5
  654.7 5.2 copy-start.3
  663.5 5.0 copy-start.10
Sparse Core Ops, SparseCore 0:
  8.9 152.3 all-gather.5
  412.8 26.1 all-gather.9
  440.8 27.8 all-gather.7
  676.8 290.5 reduce-scatter.1
where the time goes:
time: 987 us; the launch traced here: 978 us
  waiting for transfers between devices  463 us (47%)
  matrix products  404 us (41%)
  other arithmetic  55.2 us (6%)
  local copies, waits for them, and re-layouts  39 us (4%)
  between operations  13.9 us (1%)
    reduce_scatter x1, waiting for transfers between devices, body(): lax.psum_scatter(jnp.dot(piece, w_out, preferred_element_type=jnp.float32...  291 us
    dot_general x172, matrix products, mat(): return jnp.einsum('...ij,...jk->...ik', left, right, precision=highest)  179 us
    all_gather x1, waiting for transfers between devices, body(): piece = lax.all_gather(tokens, 'head', axis=0, tiled=True)  154 us
    dot_general x96, matrix products, mat_t(): return jnp.einsum('...ji,...jk->...ik', left, right, precision=highest)  149 us
    dot_general x33, matrix products, gram_bt(): jnp.einsum('...ij,...kj->...ik', left, right, preferred_element_type=jnp....  33.9 us
  transfers between devices with their start and end apart: 4, of which 3 were waited for; matrix products, arithmetic and copies ran while one was open for 4% of the time, Pallas kernels for 0%

commit v1 on v0

v1 whole, which is shorter than its diff:
```python
import functools

import jax
import jax.numpy as jnp
from jax import lax
from jax.experimental import pallas as pl
from jax.experimental.pallas import tpu as pltpu
from jax.sharding import PartitionSpec as P

CHUNK = 256
LANES = 128
VMEM = 48 * 2**20
half = jnp.bfloat16
single = jnp.float32


def mm(left, right):
    return jnp.dot(left.astype(half), right.astype(half), preferred_element_type=single)


def mm_bt(left, right):
    return lax.dot_general(left, right, (((1,), (1,)), ((), ())), preferred_element_type=single)


def mm_t(left, right):
    return lax.dot_general(
        left, right.astype(half), (((0,), (0,)), ((), ())), preferred_element_type=single
    )


def unit(raw):
    return (raw * lax.rsqrt(jnp.sum(raw * raw, -1, keepdims=True) + 1e-06)).astype(half)


def chunk_kernel(heads, tok, wq, wk, wv, wb, gain, reads_ref, outs_ref, trans_ref):
    width = wq.shape[1] // heads
    x = tok[0]
    each = range(heads)

    def project(w):
        full = jnp.dot(x, w[...], preferred_element_type=single).astype(half).astype(single)
        return [full[:, h * width : (h + 1) * width] for h in each]

    k = [unit(a) for a in project(wk)]
    beta = gain[...] * jax.nn.sigmoid(jnp.dot(x, wb[...], preferred_element_type=single))
    rates = [beta[:, h : h + 1] for h in each]
    row = lax.broadcasted_iota(jnp.int32, (CHUNK, CHUNK), 0)
    col = lax.broadcasted_iota(jnp.int32, (CHUNK, CHUNK), 1)
    near = (row // 16) == (col // 16)
    mid = (row // 64) == (col // 64)
    below = row > col
    eye = jnp.where(row == col, 1.0, 0.0).astype(single)
    lower = [jnp.where(below, rates[h] * mm_bt(k[h], k[h]), 0.0) for h in each]
    power = [jnp.where(near, a, 0.0) for a in lower]
    inverse = [eye - a for a in power]
    for level in range(3):
        power = [mm(a, a) for a in power]
        inverse = [t + mm(t, a) for t, a in zip(inverse, power)]
    rest = [mm(t, jnp.where(mid & ~near, a, 0.0)) for t, a in zip(inverse, lower)]
    inverse = [t - mm(r, t) for r, t in zip(rest, inverse)]
    rest = [mm(r, r) for r in rest]
    inverse = [t + mm(r, t) for r, t in zip(rest, inverse)]
    rest = [mm(t, jnp.where(mid, 0.0, a)) for t, a in zip(inverse, lower)]
    v = project(wv)
    terms = [jnp.concatenate([rates[h] * k[h].astype(single), rates[h] * v[h]], 1) for h in each]
    terms = [mm(t, a) for t, a in zip(inverse, terms)]
    terms = [t - mm(r, t) for r, t in zip(rest, terms)]
    rest = [mm(r, r) for r in rest]
    terms = [(t + mm(r, t)).astype(half) for r, t in zip(rest, terms)]
    q = [unit(a) for a in project(wq)]
    for h in each:
        causal = jnp.where(below | (row == col), mm_bt(q[h], k[h]), 0.0)
        read = mm(causal, terms[h])
        here = slice(h * width, (h + 1) * width)
        reads_ref[0, :, here] = (q[h].astype(single) - read[:, :width]).astype(half)
        outs_ref[0, :, here] = read[:, width:]
        trans_ref[0, h] = mm_t(k[h], terms[h])


def chunk_terms(tokens, wq, wk, wv, wb, gain, heads):
    chunks, _, depth = tokens.shape
    per = wq.shape[1]
    width = per // heads

    def once(shape):
        return pl.BlockSpec(shape, lambda i: (0,) * len(shape), pipeline_mode=pl.Buffered(1))

    return pl.pallas_call(
        functools.partial(chunk_kernel, heads),
        grid=(chunks,),
        in_specs=[pl.BlockSpec((1, CHUNK, depth), lambda i: (i, 0, 0))]
        + [once(w.shape) for w in (wq, wk, wv, wb, gain)],
        out_specs=[
            pl.BlockSpec((1, CHUNK, per), lambda i: (i, 0, 0)),
            pl.BlockSpec((1, CHUNK, per), lambda i: (i, 0, 0)),
            pl.BlockSpec((1, heads, width, 2 * width), lambda i: (i, 0, 0, 0)),
        ],
        out_shape=[
            jax.ShapeDtypeStruct((chunks, CHUNK, per), half),
            jax.ShapeDtypeStruct((chunks, CHUNK, per), single),
            jax.ShapeDtypeStruct((chunks, heads, width, 2 * width), single),
        ],
        compiler_params=pltpu.CompilerParams(vmem_limit_bytes=VMEM),
        cost_estimate=pl.CostEstimate(
            flops=2 * chunks * CHUNK * (depth * 3 * per + heads * 18 * CHUNK * CHUNK),
            bytes_accessed=2 * depth * 3 * per + chunks * CHUNK * (2 * depth + 8 * per),
            transcendentals=0,
        ),
        name="chunk_terms",
    )(tokens, wq, wk, wv, wb, gain)


def fold_kernel(parts, *refs):
    trans, (starts_ref, last_ref) = refs[:parts], refs[parts:]
    chunks, heads, width, _ = trans[0].shape
    row = lax.broadcasted_iota(jnp.int32, (width, 2 * width), 0)
    col = lax.broadcasted_iota(jnp.int32, (width, 2 * width), 1)
    state = [jnp.where(row == col, 1.0, 0.0).astype(single) for _ in range(heads)]
    for place in range(chunks):
        for part in range(parts):
            for h in range(heads):
                starts_ref[place, part, h] = state[h]
                step = trans[part][place, h]
                moved = state[h] - mm(step[:, :width], state[h])
                state[h] = moved + jnp.where(col < width, 0.0, step)
    for h in range(heads):
        last_ref[h] = state[h].astype(half)


def fold(trans):
    chunks, heads, width, wide = trans[0].shape
    parts = len(trans)
    return pl.pallas_call(
        functools.partial(fold_kernel, parts),
        out_shape=[
            jax.ShapeDtypeStruct((chunks, parts, heads, width, wide), single),
            jax.ShapeDtypeStruct((heads, width, wide), half),
        ],
        compiler_params=pltpu.CompilerParams(vmem_limit_bytes=VMEM),
        name="fold",
    )(*trans)


def emit_kernel(parts, place_ref, all_ref, starts_ref, gain, *refs):
    reads, outs, results, entry = (
        refs[:parts],
        refs[parts : 2 * parts],
        refs[2 * parts : 3 * parts],
        refs[3 * parts],
    )
    heads, width, _ = entry.shape

    @pl.when(pl.program_id(0) == 0)
    def _():
        entry[...] = jnp.zeros_like(entry)

        def one(turn, carry):
            for h in range(heads):
                pair = all_ref[turn, h]
                entry[h] = mm(pair[:, :width], entry[h]) + pair[:, width:].astype(single)
            return carry

        lax.fori_loop(0, place_ref[0], one, 0)

    for part in range(parts):
        for h in range(heads):
            here = slice(h * width, (h + 1) * width)
            pair = starts_ref[0, part, h]
            state = mm(pair[:, :width], entry[h]) + pair[:, width:]
            o = mm(reads[part][0, :, here], state) + outs[part][0, :, here]
            scale = lax.rsqrt(jnp.mean(o * o, -1, keepdims=True) + 1e-05)
            results[part][0, :, here] = (o * scale * gain[:, here]).astype(half)


def emit(place, everyone, starts, gain, reads, outs):
    parts = len(reads)
    chunks, _, per = reads[0].shape
    _, _, heads, width, wide = starts.shape
    rows = pl.BlockSpec((1, CHUNK, per), lambda i: (i, 0, 0))
    return pl.pallas_call(
        functools.partial(emit_kernel, parts),
        grid=(chunks,),
        in_specs=[
            pl.BlockSpec(memory_space=pltpu.SMEM),
            pl.BlockSpec(
                everyone.shape, lambda i: (0, 0, 0, 0), pipeline_mode=pl.Buffered(1)
            ),
            pl.BlockSpec((1, parts, heads, width, wide), lambda i: (i, 0, 0, 0, 0)),
            pl.BlockSpec((1, per), lambda i: (0, 0)),
        ]
        + [rows] * (2 * parts),
        out_specs=[rows] * parts,
        out_shape=[jax.ShapeDtypeStruct((chunks, CHUNK, per), half)] * parts,
        scratch_shapes=[pltpu.VMEM((heads, width, width), single)],
        compiler_params=pltpu.CompilerParams(vmem_limit_bytes=VMEM),
        name="emit",
    )(place, everyone, starts, gain, *reads, *outs)


def body(seqs, tokens, w_query, w_key, w_value, w_beta, beta_gain, norm_gain, w_out):
    per = w_query.shape[1]
    heads = w_beta.shape[1]
    place = lax.axis_index("seq")
    parts = tokens.shape[0] // CHUNK
    wb = jnp.pad(w_beta, ((0, 0), (0, LANES - heads)))
    gain = jnp.pad(beta_gain, (0, LANES - heads)).reshape(1, LANES)
    pieces = [
        lax.all_gather(tokens[part * CHUNK : (part + 1) * CHUNK], "head", axis=0)
        for part in range(parts)
    ]
    share = per // seqs
    mine = lax.dynamic_slice_in_dim(w_out, place * share, share, 0)
    mine, pieces[-1] = lax.optimization_barrier((mine, pieces[-1]))
    w_whole = lax.all_gather(mine, ("head", "seq"), axis=0, tiled=True)
    done = [chunk_terms(a, w_query, w_key, w_value, wb, gain, heads) for a in pieces]
    starts, last = fold([a[2] for a in done])
    everyone = lax.all_gather(last, "seq", axis=0)
    normed = emit(
        place.reshape(1).astype(jnp.int32),
        everyone,
        starts,
        norm_gain.reshape(1, per),
        [a[0] for a in done],
        [a[1] for a in done],
    )
    mixed = []
    for a in normed:
        rows = lax.all_to_all(a, "head", split_axis=0, concat_axis=2, tiled=True)
        rows = rows.reshape(CHUNK, -1)
        mixed.append(jnp.dot(rows, w_whole, preferred_element_type=single).astype(half))
    return jnp.concatenate(mixed, 0)


def solution(mesh):
    placed = (
        P(("seq", "head"), None),
        P(None, "head"),
        P(None, "head"),
        P(None, "head"),
        P(None, "head"),
        P("head"),
        P("head"),
        P("head", None),
    )
    return jax.shard_map(
        functools.partial(body, mesh.shape["seq"]),
        mesh=mesh,
        in_specs=placed,
        out_specs=P(("seq", "head"), None),
        check_vma=False,
    )
```

time: 987 us -> 358 us (0.36)
  matrix products: 404 us -> 8.21 us
  waiting for transfers between devices: 463 us -> 205 us
  Pallas kernels: 0 us -> 63.6 us
  other arithmetic: 55.2 us -> 1.57 us
  blocking collectives: 0 us -> 45.9 us
  local copies, waits for them, and re-layouts: 39 us -> 15.3 us
    dot_general x306 -> x2, matrix products: 404 us -> 8.21 us  [body(): jnp.dot(rows, w_whole, preferred_element_type=single).astype(half)]
    reduce_scatter x1 -> x0, waiting for transfers between devices: 291 us -> none  [body(): lax.psum_scatter(jnp.dot(piece, w_out, preferred_element_type=jnp.float32...]
    pallas_call x0 -> x4, Pallas kernels: none -> 63.6 us  [the longest x2 52.3 us: chunk_terms(): pl.pallas_call(functools.partial(chunk_kernel, heads), grid=(chunks,), in...]
    all_to_all x0 -> x1, waiting for transfers between devices: none -> 46.2 us  [body(): rows = lax.all_to_all(a, 'head', split_axis=0, concat_axis=2, tiled=True)]
    all_to_all x0 -> x1, blocking collectives: none -> 45.9 us  [body(): rows = lax.all_to_all(a, 'head', split_axis=0, concat_axis=2, tiled=True)]
    reduce_sum x3 -> x0, other arithmetic: 16.3 us -> none  [the longest x2 11.1 us: unit_norm(): return raw / jnp.sqrt(jnp.sum(raw * raw, -1, keepdims=True) + 1e-06)]
    reshape x4 -> x1, local copies, waits for them, and re-layouts: 13.4 us -> 0.01 us  [body(): gain = jnp.pad(beta_gain, (0, LANES - heads)).reshape(1, LANES)]
    all_gather x3 -> x4, waiting for transfers between devices: 171 us -> 158 us  [the longest x2 132 us: body(): lax.all_gather(tokens[part * CHUNK:(part + 1) * CHUNK], 'head', axis=0)]
  transfers between devices with their start and end apart: 4 -> 5, of which waited for: 3 -> 4; matrix products, arithmetic and copies ran while one was open for 4% -> 2% of each run, Pallas kernels for 0% -> 10%
where the time goes in v1:
time: 358 us
  waiting for transfers between devices  205 us (57%)
  Pallas kernels  63.6 us (18%)
  blocking collectives  45.9 us (13%)
  local copies, waits for them, and re-layouts  15.3 us (4%)
  between operations  13.3 us (4%)
  matrix products  8.21 us (2%)
  starting transfers between devices  4.57 us (1%)
    all_gather x2, waiting for transfers between devices, body(): lax.all_gather(tokens[part * CHUNK:(part + 1) * CHUNK], 'head', axis=0)  132 us
    pallas_call x2, Pallas kernels, chunk_terms(): pl.pallas_call(functools.partial(chunk_kernel, heads), grid=(chunks,), in...  52.3 us
    all_to_all x1, waiting for transfers between devices, body(): rows = lax.all_to_all(a, 'head', split_axis=0, concat_axis=2, tiled=True)  46.2 us
    all_to_all x1, blocking collectives, body(): rows = lax.all_to_all(a, 'head', split_axis=0, concat_axis=2, tiled=True)  45.9 us
    all_gather x1, waiting for transfers between devices, body(): everyone = lax.all_gather(last, 'seq', axis=0)  26 us
    dot_general x2, matrix products, body(): jnp.dot(rows, w_whole, preferred_element_type=single).astype(half)  8.21 us
    pallas_call x1, Pallas kernels, emit(): pl.pallas_call(functools.partial(emit_kernel, parts), grid=(chunks,), in_...  7.92 us
  transfers between devices with their start and end apart: 5, of which 4 were waited for; matrix products, arithmetic and copies ran while one was open for 2% of the time, Pallas kernels for 10%

profile of v1, /device:TPU:0, one launch (start us, length us, event | category | flops | bytes accessed | tf_op | source)
XLA Modules:
  0.0 357.6 jit_solution(6652485826723861666)
XLA Ops:
  6.5 0.0 copy-start
  6.5 0.0 all-gather.12.cloned.1.call-start
  6.5 3.3 fusion
  9.9 0.0 copy-start.12
  9.9 0.0 copy-start.13
  9.9 0.0 all-gather.12.cloned.1.call-update
  9.9 0.0 all-gather.10.cloned.1.call-start
  9.9 0.7 all-gather.10.cloned.1.call-update
  10.6 0.0 all-gather.14.cloned.1.call-start
  10.7 0.0 copy-done.12
  10.7 0.3 copy.13
  11.0 0.9 pad.8.wb
  11.9 0.0 copy-done.13
  11.9 0.0 copy-done
  11.9 0.7 constant_dynamic-slice_fusion
  12.6 80.9 %all-gather.12.cloned.1.call-done = bf16[1024,2048]{1,0:T(8,128)(2,1)} async-done(((bf16[256,2048]{1,0:T(8,128)(2,1)}), bf16[1024,2048]{1,0:T(8,128)(2,1)}) %all-gather.12.cloned.1.call-update) | async-done | bytes 4194320 | tf_op jit(solution)/shard_map/all_gather | solution.py:208
  93.5 0.0 copy-start.7
  93.5 1.0 copy-done.7
  94.5 26.1 %chunk_terms.3 = (bf16[4,256,512]{2,1,0:T(8,128)(2,1)S(1)}, f32[4,256,512]{2,1,0:T(8,128)S(1)}, f32[4,4,128,256]{3,2,1,0:T(8,128)S(1)}) custom-call(bf16[4,256,2048]{2,1,0:T(8,128)(2,1)} %bitcast.24, bf16[2048,512]{1,0:T(8,128)(2,1)} %wq.3, bf16[2048,512]{1,0:T(8,128)(2,1)} %wk.3, bf16[2048,512]{1,0:T(8,128)(2,1)} %wv.3, bf16[2048,128]{1,0:T(8,128)(2,1)S(1)} %copy-done.7, ...), custom_call_target="tpu_custom_call" | custom-call | flops 16106127360 | bytes 14680064 | tf_op jit(solution)/shard_map/chunk_terms/pallas_call | solution.py:88
  120.6 0.0 copy-start.1
  120.6 1.3 copy-done.1
  122.0 0.0 copy-start.3
  122.0 1.3 copy-done.3
  123.3 51.1 %all-gather.10.cloned.1.call-done = bf16[1024,2048]{1,0:T(8,128)(2,1)} async-done(((bf16[256,2048]{1,0:T(8,128)(2,1)}), bf16[1024,2048]{1,0:T(8,128)(2,1)}) %all-gather.10.cloned.1.call-update) | async-done | bytes 4194320 | tf_op jit(solution)/shard_map/all_gather | solution.py:208
  174.4 0.0 copy-start.8
  174.4 1.0 copy-done.8
  175.4 0.0 copy-start.2
  175.4 26.2 %chunk_terms.2 = (bf16[4,256,512]{2,1,0:T(8,128)(2,1)S(1)}, f32[4,256,512]{2,1,0:T(8,128)S(1)}, f32[4,4,128,256]{3,2,1,0:T(8,128)S(1)}) custom-call(bf16[4,256,2048]{2,1,0:T(8,128)(2,1)} %bitcast.25, bf16[2048,512]{1,0:T(8,128)(2,1)} %wq.3, bf16[2048,512]{1,0:T(8,128)(2,1)} %wk.3, bf16[2048,512]{1,0:T(8,128)(2,1)} %wv.3, bf16[2048,128]{1,0:T(8,128)(2,1)S(1)} %copy-done.8, ...), custom_call_target="tpu_custom_call" | custom-call | flops 16106127360 | bytes 14680064 | tf_op jit(solution)/shard_map/chunk_terms/pallas_call | solution.py:88
  201.7 0.0 copy-start.4
  201.7 0.0 copy-start.5
  201.7 0.0 copy-done.2
  201.7 0.0 copy-start.9
  201.7 3.3 fold.1
  205.0 0.0 copy-done.4
  205.0 0.0 copy-done.5
  205.0 0.0 all-gather.14.cloned.1.call-update
  205.1 0.2 all-gather.8.cloned.1.call-start
  205.3 0.3 all-gather.8.cloned.1.call-update
  205.7 26.0 %all-gather.14.cloned.1.call-done = bf16[32,128,256]{2,1,0:T(8,128)(2,1)} async-done(((bf16[4,128,256]{2,1,0:T(8,128)(2,1)}), bf16[32,128,256]{2,1,0:T(8,128)(2,1)}) %all-gather.14.cloned.1.call-update) | async-done | bytes 2097168 | tf_op jit(solution)/shard_map/all_gather | solution.py:217
  231.6 0.0 copy-done.9
  231.6 0.0 copy-start.6
  231.6 1.2 copy-done.6
  232.9 7.9 %emit.1 = (bf16[4,256,512]{2,1,0:T(8,128)(2,1)S(1)}, bf16[4,256,512]{2,1,0:T(8,128)(2,1)}) custom-call(s32[1]{0:T(128)} %bitcast.place_ref, bf16[8,4,128,256]{3,2,1,0:T(8,128)(2,1)} %bitcast.23, f32[4,2,4,128,256]{4,3,2,1,0:T(8,128)} %get-tuple-element.21.starts_ref, f32[1,512]{1,0:T(1,128)S(1)} %bitcast.19, bf16[4,256,512]{2,1,0:T(8,128)(2,1)S(1)} %copy-done.6, ...), custom_call_target="tpu_custom_call" | custom-call | tf_op jit(solution)/shard_map/emit/pallas_call | solution.py:180
  240.8 45.9 %all_to_all.30 = bf16[4,256,512]{2,1,0:T(8,128)(2,1)} all-to-all(bf16[4,256,512]{2,1,0:T(8,128)(2,1)S(1)} %get-tuple-element.26), channel_id=1, replica_groups=mesh['seq'=8,'head'=4] {'head'}, dimensions={0} | all-to-all | bytes 2097152 | tf_op jit(solution)/shard_map/all_to_all | solution.py:228
  286.7 4.3 %all-to-all-start.1 = ((bf16[4,256,512]{2,1,0:T(8,128)(2,1)}), bf16[4,256,512]{2,1,0:T(8,128)(2,1)}, u32[]{:S(2)}, u32[]{:S(2)}) async-start(bf16[4,256,512]{2,1,0:T(8,128)(2,1)} %get-tuple-element.28), calls=%async_computation.1 | async-start | bytes 2097152 | tf_op jit(solution)/shard_map/all_to_all | solution.py:228
  290.9 1.7 copy.14
  292.7 46.2 %all-to-all-done.1 = bf16[4,256,512]{2,1,0:T(8,128)(2,1)} async-done(((bf16[4,256,512]{2,1,0:T(8,128)(2,1)}), bf16[4,256,512]{2,1,0:T(8,128)(2,1)}, u32[]{:S(2)}, u32[]{:S(2)}) %all-to-all-start.1) | async-done | bytes 1048608 | tf_op jit(solution)/shard_map/all_to_all | solution.py:228
  338.9 2.3 copy.15
  341.1 0.0 all-gather.8.cloned.1.call-done
  341.1 0.0 copy-start.10
  341.1 0.0 copy-start.11
  341.1 5.9 %convolution_convert_fusion.1 = bf16[256,2048]{1,0:T(8,128)(2,1)S(1)} fusion(bf16[256,2048]{0,1:T(8,128)(2,1)S(1)} %bitcast.20, bf16[2048,2048]{1,0:T(8,128)(2,1)} %all-gather.8.cloned.1.call-done), kind=kOutput, calls=%fused_computation.1 | convolution fusion | flops 2148007936 | bytes 10485760 | tf_op jit(solution)/shard_map/dot_general | solution.py:230
  347.0 0.0 copy-done.10
  347.0 0.1 copy-done.11
  347.1 2.3 convolution_convert_fusion
  349.5 1.6 pad_maximum_fusion
  (1 shorter events, 0.0 us)
Async XLA Ops:
  6.5 5.4 %copy-start = (bf16[512,2048]{1,0:T(8,128)(2,1)S(1)}, bf16[512,2048]{1,0:T(8,128)(2,1)}, u32[]{:S(2)}) copy-start(bf16[512,2048]{1,0:T(8,128)(2,1)} %param.15) | copy-start | bytes 6291460
  6.5 87.0 %all-gather.12.cloned.1.call-start = ((), (), s32[]{:S(2)}) async-start(), calls=%async_computation.4 | async-start | bytes 5242880 | tf_op jit(solution)/shard_map/all_gather | solution.py:208
  9.9 0.8 copy-start.12
  9.9 2.1 copy-start.13
  9.9 164.5 %all-gather.10.cloned.1.call-start = ((), (), s32[]{:S(2)}) async-start(), calls=%async_computation.3 | async-start | bytes 5242880 | tf_op jit(solution)/shard_map/all_gather | solution.py:208
  10.6 221.0 %all-gather.14.cloned.1.call-start = ((), (), s32[]{:S(2)}) async-start(), calls=%async_computation.5 | async-start | bytes 2359296 | tf_op jit(solution)/shard_map/all_gather | solution.py:217
  93.5 1.0 copy-start.7
  120.6 1.3 copy-start.1
  122.0 1.3 copy-start.3
  174.4 1.0 copy-start.8
  175.4 26.2 %copy-start.2 = (f32[4,4,128,256]{3,2,1,0:T(8,128)S(1)}, f32[4,4,128,256]{3,2,1,0:T(8,128)}, u32[]{:S(2)}) copy-start(f32[4,4,128,256]{3,2,1,0:T(8,128)} %copy-done.1) | copy-start | bytes 6291460
  201.7 3.4 copy-start.4
  201.7 3.4 copy-start.5
  201.7 30.0 %copy-start.9 = (f32[512]{0:T(512)S(1)}, f32[512]{0:T(512)}, u32[]{:S(2)}) copy-start(f32[512]{0:T(512)} %param.14) | copy-start | bytes 6148
  205.1 136.1 %all-gather.8.cloned.1.call-start = ((), (), s32[]{:S(2)}) async-start(), calls=%async_computation.2 | async-start | bytes 8650752 | tf_op jit(solution)/shard_map/all_gather | solution.py:214
  231.6 1.2 copy-start.6
  286.7 52.2 %all-to-all-start.1 = ((bf16[4,256,512]{2,1,0:T(8,128)(2,1)}), bf16[4,256,512]{2,1,0:T(8,128)(2,1)}, u32[]{:S(2)}, u32[]{:S(2)}) async-start(bf16[4,256,512]{2,1,0:T(8,128)(2,1)} %get-tuple-element.28), calls=%async_computation.1 | async-start | bytes 2097152 | tf_op jit(solution)/shard_map/all_to_all | solution.py:228
  341.1 5.9 %copy-start.10 = (bf16[2048,2048]{1,0:T(8,128)(2,1)S(1)}, bf16[2048,2048]{1,0:T(8,128)(2,1)}, u32[]{:S(2)}) copy-start(bf16[2048,2048]{1,0:T(8,128)(2,1)} %all-gather.8.cloned.1.call-done) | copy-start | bytes 25165828
  341.1 6.0 %copy-start.11 = (bf16[1,256,4,512]{1,3,2,0:T(8,128)(2,1)S(1)}, bf16[1,256,4,512]{1,3,2,0:T(8,128)(2,1)}, u32[]{:S(2)}) copy-start(bf16[1,256,4,512]{1,3,2,0:T(8,128)(2,1)} %copy.15) | copy-start | bytes 3145732
Sparse Core Ops, SparseCore 0:
  10.0 83.4 all-gather.11
  95.1 79.2 all-gather.9
  205.2 26.4 all-gather.13
  234.4 106.3 all-gather.7

commit v2 on v1

--- a/solution.py
+++ b/solution.py
@@ -77,10 +77,14 @@
         trans_ref[0, h] = mm_t(k[h], terms[h])
 
 
-def chunk_terms(tokens, wq, wk, wv, wb, gain, heads):
+def chunk_terms(tokens, wq, wk, wv, wb, gain, heads, group):
     chunks, _, depth = tokens.shape
-    per = wq.shape[1]
-    width = per // heads
+    width = wq.shape[1] // wb.shape[1]
+    per = heads * width
+    gain = jnp.pad(gain[group * heads : (group + 1) * heads], (0, LANES - heads))
+    gain = gain.reshape(1, LANES)
+    wb = wb[:, group * heads : (group + 1) * heads]
+    wb = jnp.pad(wb, ((0, 0), (0, LANES - heads)))
 
     def once(shape):
         return pl.BlockSpec(shape, lambda i: (0,) * len(shape), pipeline_mode=pl.Buffered(1))
@@ -89,7 +93,11 @@
         functools.partial(chunk_kernel, heads),
         grid=(chunks,),
         in_specs=[pl.BlockSpec((1, CHUNK, depth), lambda i: (i, 0, 0))]
-        + [once(w.shape) for w in (wq, wk, wv, wb, gain)],
+        + [
+            pl.BlockSpec((depth, per), lambda i: (0, group), pipeline_mode=pl.Buffered(1))
+            for _ in range(3)
+        ]
+        + [once(w.shape) for w in (wb, gain)],
         out_specs=[
             pl.BlockSpec((1, CHUNK, per), lambda i: (i, 0, 0)),
             pl.BlockSpec((1, CHUNK, per), lambda i: (i, 0, 0)),
@@ -142,12 +150,7 @@
 
 
 def emit_kernel(parts, place_ref, all_ref, starts_ref, gain, *refs):
-    reads, outs, results, entry = (
-        refs[:parts],
-        refs[parts : 2 * parts],
-        refs[2 * parts : 3 * parts],
-        refs[3 * parts],
-    )
+    reads, outs, (result, entry) = refs[:parts], refs[parts : 2 * parts], refs[2 * parts :]
     heads, width, _ = entry.shape
 
     @pl.when(pl.program_id(0) == 0)
@@ -169,7 +172,8 @@
             state = mm(pair[:, :width], entry[h]) + pair[:, width:]
             o = mm(reads[part][0, :, here], state) + outs[part][0, :, here]
             scale = lax.rsqrt(jnp.mean(o * o, -1, keepdims=True) + 1e-05)
-            results[part][0, :, here] = (o * scale * gain[:, here]).astype(half)
+            rows = slice(part * CHUNK, (part + 1) * CHUNK)
+            result[0, rows, here] = (o * scale * gain[:, here]).astype(half)
 
 
 def emit(place, everyone, starts, gain, reads, outs):
@@ -189,46 +193,102 @@
             pl.BlockSpec((1, per), lambda i: (0, 0)),
         ]
         + [rows] * (2 * parts),
-        out_specs=[rows] * parts,
-        out_shape=[jax.ShapeDtypeStruct((chunks, CHUNK, per), half)] * parts,
+        out_specs=pl.BlockSpec((1, parts * CHUNK, per), lambda i: (i, 0, 0)),
+        out_shape=jax.ShapeDtypeStruct((chunks, parts * CHUNK, per), half),
         scratch_shapes=[pltpu.VMEM((heads, width, width), single)],
         compiler_params=pltpu.CompilerParams(vmem_limit_bytes=VMEM),
         name="emit",
     )(place, everyone, starts, gain, *reads, *outs)
 
 
-def body(seqs, tokens, w_query, w_key, w_value, w_beta, beta_gain, norm_gain, w_out):
+def mix_kernel(groups, *refs):
+    rows, (w, out) = refs[:groups], refs[groups:]
+    owners, _, width = rows[0].shape
+    total = 0.0
+    for owner in range(owners):
+        for g in range(groups):
+            first = (owner * groups + g) * width
+            total += mm(rows[g][owner], w[first : first + width, :])
+    out[...] = total.astype(half)
+
+
+def mix(rows, w_whole):
+    depth, columns = w_whole.shape
+    count = rows[0].shape[1]
+    tile = 512
+    return pl.pallas_call(
+        functools.partial(mix_kernel, len(rows)),
+        grid=(columns // tile,),
+        in_specs=[pl.BlockSpec(a.shape, lambda i: (0, 0, 0)) for a in rows]
+        + [pl.BlockSpec((depth, tile), lambda i: (0, i))],
+        out_specs=pl.BlockSpec((count, tile), lambda i: (0, i)),
+        out_shape=jax.ShapeDtypeStruct((count, columns), half),
+        compiler_params=pltpu.CompilerParams(vmem_limit_bytes=VMEM),
+        name="mix",
+    )(*rows, w_whole)
+
+
+def whole_weight(w_out, seqs, owners):
+    per, columns = w_out.shape
+    place = lax.axis_index("seq")
+    share = per // seqs
+    mine = lax.dynamic_slice_in_dim(w_out, place * share, share, 0)
+    turned = [mine]
+    for shift in range(1, owners):
+        pairs = [(i, (i + shift) % owners) for i in range(owners)]
+        turned.append(lax.ppermute(mine, "head", pairs))
+    turned = jnp.stack(turned)
+    owner = lax.axis_index("head")
+    held = jnp.stack(
+        [
+            lax.dynamic_index_in_dim(turned, (owner - i + owners) % owners, 0, False)
+            for i in range(owners)
+        ]
+    )
+    levels = seqs.bit_length() - 1
+    turns = list(range(1, levels)) + [0]
+    for bit in turns:
+        pairs = [(i, i ^ (1 << bit)) for i in range(seqs)]
+        other = lax.ppermute(held, "seq", pairs)
+        upper = (place >> bit) & 1 == 1
+        held = jnp.stack([jnp.where(upper, other, held), jnp.where(upper, held, other)])
+    axes = [turns[::-1].index(bit) for bit in reversed(range(levels))]
+    held = held.transpose([levels] + axes + [levels + 1, levels + 2])
+    return held.reshape(owners * per, columns)
+
+
+def body(seqs, owners, tokens, w_query, w_key, w_value, w_beta, beta_gain, norm_gain, w_out):
     per = w_query.shape[1]
     heads = w_beta.shape[1]
     place = lax.axis_index("seq")
     parts = tokens.shape[0] // CHUNK
-    wb = jnp.pad(w_beta, ((0, 0), (0, LANES - heads)))
-    gain = jnp.pad(beta_gain, (0, LANES - heads)).reshape(1, LANES)
+    groups = 2
+    few = heads // groups
+    w_whole = whole_weight(w_out, seqs, owners)
     pieces = [
         lax.all_gather(tokens[part * CHUNK : (part + 1) * CHUNK], "head", axis=0)
         for part in range(parts)
     ]
-    share = per // seqs
-    mine = lax.dynamic_slice_in_dim(w_out, place * share, share, 0)
-    mine, pieces[-1] = lax.optimization_barrier((mine, pieces[-1]))
-    w_whole = lax.all_gather(mine, ("head", "seq"), axis=0, tiled=True)
-    done = [chunk_terms(a, w_query, w_key, w_value, wb, gain, heads) for a in pieces]
-    starts, last = fold([a[2] for a in done])
-    everyone = lax.all_gather(last, "seq", axis=0)
-    normed = emit(
-        place.reshape(1).astype(jnp.int32),
-        everyone,
-        starts,
-        norm_gain.reshape(1, per),
-        [a[0] for a in done],
-        [a[1] for a in done],
-    )
-    mixed = []
-    for a in normed:
-        rows = lax.all_to_all(a, "head", split_axis=0, concat_axis=2, tiled=True)
-        rows = rows.reshape(CHUNK, -1)
-        mixed.append(jnp.dot(rows, w_whole, preferred_element_type=single).astype(half))
-    return jnp.concatenate(mixed, 0)
+    weights = (w_query, w_key, w_value, w_beta, beta_gain)
+    done = []
+    for a in pieces:
+        if done:
+            a, done[-1] = lax.optimization_barrier((a, done[-1]))
+        done.append([chunk_terms(a, *weights, few, g) for g in range(groups)])
+    pairs = [fold([a[g][2] for a in done]) for g in range(groups)]
+    everyone = [lax.all_gather(last, "seq", axis=0) for _, last in pairs]
+    rows = []
+    for g in range(groups):
+        normed = emit(
+            place.reshape(1).astype(jnp.int32),
+            everyone[g],
+            pairs[g][0],
+            norm_gain[g * per // groups : (g + 1) * per // groups].reshape(1, -1),
+            [a[g][0] for a in done],
+            [a[g][1] for a in done],
+        )
+        rows.append(lax.all_to_all(normed, "head", split_axis=0, concat_axis=0, tiled=True))
+    return mix(rows, w_whole)
 
 
 def solution(mesh):
@@ -243,7 +303,7 @@
         P("head", None),
     )
     return jax.shard_map(
-        functools.partial(body, mesh.shape["seq"]),
+        functools.partial(body, mesh.shape["seq"], mesh.shape["head"]),
         mesh=mesh,
         in_specs=placed,
         out_specs=P(("seq", "head"), None),

time: 358 us -> 327 us (0.913)
  waiting for transfers between devices: 205 us -> 138 us
  blocking collectives: 45.9 us -> 0 us
  Pallas kernels: 63.6 us -> 96.6 us
  local copies, waits for them, and re-layouts: 15.3 us -> 42.4 us
  other arithmetic: 1.57 us -> 19.1 us
  starting transfers between devices: 4.57 us -> 16.5 us
  matrix products: 8.21 us -> 0 us
    all_gather x2, waiting for transfers between devices: 132 us -> 25.1 us  [body(): lax.all_gather(tokens[part * CHUNK:(part + 1) * CHUNK], 'head', axis=0)]
    ppermute x0 -> x6, waiting for transfers between devices: none -> 90.9 us  [the longest x3 52.7 us: whole_weight(): other = lax.ppermute(held, 'seq', pairs)]
    all_to_all x1 -> x0, blocking collectives: 45.9 us -> none  [body(): rows = lax.all_to_all(a, 'head', split_axis=0, concat_axis=2, tiled=True)]
    all_to_all x1 -> x2, waiting for transfers between devices: 46.2 us -> 11.3 us  [body(): lax.all_to_all(normed, 'head', split_axis=0, concat_axis=0, tiled=True)]
    pallas_call x2 -> x4, Pallas kernels: 52.3 us -> 74.8 us  [chunk_terms(): pl.pallas_call(functools.partial(chunk_kernel, heads), grid=(chunks,), in...]
    unnamed x29 -> x74, local copies, waits for them, and re-layouts: 6.37 us -> 28.3 us
    all_gather x2, waiting for transfers between devices: 26 us -> 10.3 us  [body(): everyone = [lax.all_gather(last, 'seq', axis=0) for _, last in pairs]]
    another operation x0 -> x7, other arithmetic: none -> 11.6 us  [the longest x5 11.3 us: whole_weight(): jnp.stack([jnp.where(upper, other, held), jnp.where(upper, held, other)])]
  transfers between devices with their start and end apart: 5 -> 12, of which waited for: 4 -> 8; matrix products, arithmetic and copies ran while one was open for 2% -> 10% of each run, Pallas kernels for 10% -> 27%
where the time goes in v2:
time: 327 us; the launch traced here: 326 us
  waiting for transfers between devices  138 us (42%)
  Pallas kernels  96.6 us (30%)
  local copies, waits for them, and re-layouts  42.4 us (13%)
  other arithmetic  19.1 us (6%)
  starting transfers between devices  16.5 us (5%)
  between operations  13.4 us (4%)
    pallas_call x4, Pallas kernels, chunk_terms(): pl.pallas_call(functools.partial(chunk_kernel, heads), grid=(chunks,), in...  74.8 us
    ppermute x3, waiting for transfers between devices, whole_weight(): other = lax.ppermute(held, 'seq', pairs)  52.7 us
    ppermute x3, waiting for transfers between devices, whole_weight(): turned.append(lax.ppermute(mine, 'head', pairs))  38.2 us
    unnamed x74, local copies, waits for them, and re-layouts  28.3 us
    all_gather x2, waiting for transfers between devices, body(): lax.all_gather(tokens[part * CHUNK:(part + 1) * CHUNK], 'head', axis=0)  25.1 us
    another operation x5, other arithmetic, whole_weight(): jnp.stack([jnp.where(upper, other, held), jnp.where(upper, held, other)])  11.3 us
    all_to_all x2, waiting for transfers between devices, body(): lax.all_to_all(normed, 'head', split_axis=0, concat_axis=0, tiled=True)  11.3 us
    all_gather x2, waiting for transfers between devices, body(): everyone = [lax.all_gather(last, 'seq', axis=0) for _, last in pairs]  10.3 us
  transfers between devices with their start and end apart: 12, of which 8 were waited for; matrix products, arithmetic and copies ran while one was open for 10% of the time, Pallas kernels for 27%

profile of v2, /device:TPU:0, one launch (start us, length us, event | category | flops | bytes accessed | tf_op | source)
XLA Modules:
  0.0 325.7 jit_solution(13065496219842671437)
XLA Ops:
  6.5 3.3 %fusion = (bf16[256,2048]{1,0:T(8,128)(2,1)}, bf16[256,2048]{1,0:T(8,128)(2,1)}) fusion(bf16[512,2048]{1,0:T(8,128)(2,1)} %param.8), kind=kLoop, calls=%fused_computation.18 | loop fusion | bytes 4194304 | tf_op jit(solution)/shard_map/slice | solution.py:269
  9.9 5.1 %collective-permute-start.2 = (bf16[64,2048]{1,0:T(8,128)(2,1)S(1)}, bf16[64,2048]{1,0:T(8,128)(2,1)S(1)}, u32[]{:S(2)}, u32[]{:S(2)}) collective-permute-start(bf16[64,2048]{1,0:T(8,128)(2,1)S(1)} %constant_dynamic-slice_fusion.4), channel_id=1, source_target_pairs={{0,3},{1,0},{2,1},{3,2},{4,7},{5,4},{6,5},{7,6},{8,11},{9,8},{10,9... | collective-permute-start | bytes 786440 | tf_op jit(solution)/shard_map/ppermute | solution.py:239
  15.1 1.0 collective-permute-start
  16.1 5.9 %collective-permute-done.2 = bf16[64,2048]{1,0:T(8,128)(2,1)S(1)} collective-permute-done((bf16[64,2048]{1,0:T(8,128)(2,1)S(1)}, bf16[64,2048]{1,0:T(8,128)(2,1)S(1)}, u32[]{:S(2)}, u32[]{:S(2)}) %collective-permute-start.2) | collective-permute-done | bytes 262176 | tf_op jit(solution)/shard_map/ppermute | solution.py:239
  22.0 32.3 %collective-permute-done.1 = bf16[64,2048]{1,0:T(8,128)(2,1)S(1)} collective-permute-done((bf16[64,2048]{1,0:T(8,128)(2,1)S(1)}, bf16[64,2048]{1,0:T(8,128)(2,1)S(1)}, u32[]{:S(2)}, u32[]{:S(2)}) %collective-permute-start.1) | collective-permute-done | bytes 262176 | tf_op jit(solution)/shard_map/ppermute | solution.py:239
  54.3 0.1 pad_maximum_fusion.2
  54.4 0.1 constant_dynamic-slice_fusion.3
  54.5 0.1 pad_maximum_fusion.3
  54.7 1.6 collective-permute-start.3
  56.3 17.3 %collective-permute-done.3 = bf16[4,64,2048]{2,1,0:T(8,128)(2,1)S(1)} collective-permute-done((bf16[4,64,2048]{2,1,0:T(8,128)(2,1)S(1)}, bf16[4,64,2048]{2,1,0:T(8,128)(2,1)S(1)}, u32[]{:S(2)}, u32[]{:S(2)}) %collective-permute-start.3) | collective-permute-done | bytes 1048608 | tf_op jit(solution)/shard_map/ppermute | solution.py:252
  73.6 0.2 select_bitcast_fusion.5
  73.8 0.2 pad_maximum_fusion.1
  74.0 0.8 copy-done.31
  74.8 0.4 copy-done.32
  75.2 1.5 collective-permute-start.4
  76.7 0.3 copy.15
  77.0 1.1 copy.16
  78.1 0.1 pad.18.wb
  78.2 2.2 pad.20.wb
  80.4 0.1 fusion.3
  80.4 35.4 %collective-permute-done.4 = bf16[2,4,64,2048]{3,2,1,0:T(8,128)(2,1)} collective-permute-done((bf16[2,4,64,2048]{3,2,1,0:T(8,128)(2,1)S(1)}, bf16[2,4,64,2048]{3,2,1,0:T(8,128)(2,1)}, u32[]{:S(2)}, u32[]{:S(2)}) %collective-permute-start.4) | collective-permute-done | bytes 2097184 | tf_op jit(solution)/shard_map/ppermute | solution.py:252
  115.8 2.7 select_bitcast_fusion.3
  118.6 1.3 copy-done.30
  119.9 2.4 pad_maximum_fusion
  122.3 1.6 copy-done.26
  123.9 18.7 %chunk_terms.4 = (bf16[4,256,256]{2,1,0:T(8,128)(2,1)S(1)}, f32[4,256,256]{2,1,0:T(8,128)S(1)}, f32[4,2,128,256]{3,2,1,0:T(8,128)S(1)}) custom-call(bf16[4,256,2048]{2,1,0:T(8,128)(2,1)} %bitcast.39, bf16[2048,512]{1,0:T(8,128)(2,1)S(1)} %copy-done.26, bf16[2048,512]{1,0:T(8,128)(2,1)} %wk.7, bf16[2048,512]{1,0:T(8,128)(2,1)} %wv.7, ...), custom_call_target="tpu_custom_call" | custom-call | flops 8053063680 | bytes 9437184 | tf_op jit(solution)/shard_map/chunk_terms/pallas_call | solution.py:92
  142.6 0.8 copy-done.20
  143.4 18.7 %chunk_terms.5 = (bf16[4,256,256]{2,1,0:T(8,128)(2,1)S(1)}, f32[4,256,256]{2,1,0:T(8,128)S(1)}, f32[4,2,128,256]{3,2,1,0:T(8,128)S(1)}) custom-call(bf16[4,256,2048]{2,1,0:T(8,128)(2,1)} %bitcast.40, bf16[2048,512]{1,0:T(8,128)(2,1)S(1)} %copy-done.26, bf16[2048,512]{1,0:T(8,128)(2,1)} %wk.7, bf16[2048,512]{1,0:T(8,128)(2,1)} %wv.7, ...), custom_call_target="tpu_custom_call" | custom-call | flops 8053063680 | bytes 9437184 | tf_op jit(solution)/shard_map/chunk_terms/pallas_call | solution.py:92
  162.1 1.0 copy-done.6
  163.1 0.8 copy-done.18
  163.9 25.1 %all-gather.9.cloned.1.call-done = bf16[1024,2048]{1,0:T(8,128)(2,1)} async-done(((bf16[256,2048]{1,0:T(8,128)(2,1)}), bf16[1024,2048]{1,0:T(8,128)(2,1)}) %all-gather.9.cloned.1.call-update) | async-done | bytes 4194320 | tf_op jit(solution)/shard_map/all_gather | solution.py:269
  189.0 1.0 copy-done.17
  190.0 1.6 copy-done.27
  191.6 18.7 %chunk_terms.6 = (bf16[4,256,256]{2,1,0:T(8,128)(2,1)S(1)}, f32[4,256,256]{2,1,0:T(8,128)S(1)}, f32[4,2,128,256]{3,2,1,0:T(8,128)S(1)}) custom-call(bf16[4,256,2048]{2,1,0:T(8,128)(2,1)} %bitcast.41, bf16[2048,512]{1,0:T(8,128)(2,1)S(1)} %copy-done.27, bf16[2048,512]{1,0:T(8,128)(2,1)} %wk.7, bf16[2048,512]{1,0:T(8,128)(2,1)} %wv.7, ...), custom_call_target="tpu_custom_call" | custom-call | flops 8053063680 | bytes 9437184 | tf_op jit(solution)/shard_map/chunk_terms/pallas_call | solution.py:92
  210.3 1.0 copy-done.8
  211.3 0.8 copy-done.22
  212.1 1.9 fold.2
  214.1 1.3 copy-done.4
  215.5 1.0 copy-done.15
  216.5 1.6 copy-done.28
  218.1 18.7 %chunk_terms.7 = (bf16[4,256,256]{2,1,0:T(8,128)(2,1)S(1)}, f32[4,256,256]{2,1,0:T(8,128)S(1)}, f32[4,2,128,256]{3,2,1,0:T(8,128)S(1)}) custom-call(bf16[4,256,2048]{2,1,0:T(8,128)(2,1)} %bitcast.42, bf16[2048,512]{1,0:T(8,128)(2,1)S(1)} %copy-done.28, bf16[2048,512]{1,0:T(8,128)(2,1)} %wk.7, bf16[2048,512]{1,0:T(8,128)(2,1)} %wv.7, ...), custom_call_target="tpu_custom_call" | custom-call | flops 8053063680 | bytes 9437184 | tf_op jit(solution)/shard_map/chunk_terms/pallas_call | solution.py:92
  236.8 1.0 copy-done.10
  237.8 0.8 copy-done.24
  238.6 1.9 fold.3
  240.5 1.3 copy-done.5
  241.9 1.2 copy-done.12
  243.1 1.0 copy-done.21
  244.2 1.0 copy-done.23
  245.2 4.9 %emit.2 = bf16[4,512,256]{2,1,0:T(8,128)(2,1)} custom-call(s32[1]{0:T(128)} %bitcast.place_ref, bf16[8,2,128,256]{3,2,1,0:T(8,128)(2,1)S(1)} %bitcast.31, f32[4,2,2,128,256]{4,3,2,1,0:T(8,128)} %copy-done.4, f32[1,256]{1,0:T(1,128)S(1)} %bitcast.34, bf16[4,256,256]{2,1,0:T(8,128)(2,1)S(1)} %copy-done.21, bf16[4,256,256]{2,1,0:T(8,128)(2,1)S(1)} %copy-done.23, ...), custom_call_target="tpu_custom_call" | custom-call | tf_op jit(solution)/shard_map/emit/pallas_call | solution.py:184
  250.1 3.6 %all-to-all-start = ((bf16[4,512,256]{2,1,0:T(8,128)(2,1)}), bf16[4,512,256]{2,1,0:T(8,128)(2,1)S(1)}, u32[]{:S(2)}, u32[]{:S(2)}) async-start(bf16[4,512,256]{2,1,0:T(8,128)(2,1)} %emit.2), calls=%async_computation | async-start | bytes 2097152 | tf_op jit(solution)/shard_map/all_to_all | solution.py:290
  253.7 10.3 %all-gather.15.cloned.1.call-done = bf16[16,128,256]{2,1,0:T(8,128)(2,1)} async-done(((bf16[2,128,256]{2,1,0:T(8,128)(2,1)}), bf16[16,128,256]{2,1,0:T(8,128)(2,1)}) %all-gather.15.cloned.1.call-update) | async-done | bytes 1048592 | tf_op jit(solution)/shard_map/all_gather | solution.py:279
  264.0 1.2 copy-done.13
  265.3 1.0 copy-done.19
  266.3 1.0 copy-done.25
  267.4 4.9 %emit.3 = bf16[4,512,256]{2,1,0:T(8,128)(2,1)} custom-call(s32[1]{0:T(128)} %bitcast.place_ref, bf16[8,2,128,256]{3,2,1,0:T(8,128)(2,1)S(1)} %bitcast.32, f32[4,2,2,128,256]{4,3,2,1,0:T(8,128)} %copy-done.5, f32[1,256]{1,0:T(1,128)S(1)} %bitcast.33, bf16[4,256,256]{2,1,0:T(8,128)(2,1)S(1)} %copy-done.19, bf16[4,256,256]{2,1,0:T(8,128)(2,1)S(1)} %copy-done.25, ...), custom_call_target="tpu_custom_call" | custom-call | tf_op jit(solution)/shard_map/emit/pallas_call | solution.py:184
  272.2 7.7 %all-to-all-done.refs_0_ = bf16[4,512,256]{2,1,0:T(8,128)(2,1)S(1)} async-done(((bf16[4,512,256]{2,1,0:T(8,128)(2,1)}), bf16[4,512,256]{2,1,0:T(8,128)(2,1)S(1)}, u32[]{:S(2)}, u32[]{:S(2)}) %all-to-all-start) | async-done | bytes 1048608 | tf_op jit(solution)/shard_map/all_to_all | solution.py:290
  279.9 3.5 %all-to-all-start.1 = ((bf16[4,512,256]{2,1,0:T(8,128)(2,1)}), bf16[4,512,256]{2,1,0:T(8,128)(2,1)S(1)}, u32[]{:S(2)}, u32[]{:S(2)}) async-start(bf16[4,512,256]{2,1,0:T(8,128)(2,1)} %emit.3), calls=%async_computation.1 | async-start | bytes 2097152 | tf_op jit(solution)/shard_map/all_to_all | solution.py:290
  283.4 5.8 %select_bitcast_fusion.1 = (bf16[1,2,2,4,64,2048]{5,4,3,2,1,0:T(8,128)(2,1)}, bf16[1,2,2,4,64,2048]{5,4,3,2,1,0:T(8,128)(2,1)}) fusion(bf16[2,2,4,64,2048]{4,3,2,1,0:T(8,128)(2,1)} %collective-permute-done.5, pred[]{:T(512)S(6)} %eq.14, bf16[1,2,4,64,2048]{4,3,2,1,0:T(8,128)(2,1)} %copy-done.30, bf16[1,2,4,64,2048]{4,3,2,1,0:T(8,128)(2,1)} %copy-done.29), kind=kLoop, calls=%fused_computation.3 | loop fusion | flops 6291456 | bytes 16777216 | tf_op jit(solution)/shard_map/stack | solution.py:254
  289.2 7.6 %maximum_bitcast_fusion = bf16[4,2,2,2,64,2048]{5,4,0,2,1,3:T(8,128)(2,1)} fusion(bf16[1,2,2,4,64,2048]{5,4,3,2,1,0:T(8,128)(2,1)} %get-tuple-element.52, bf16[1,2,2,4,64,2048]{5,4,3,2,1,0:T(8,128)(2,1)} %get-tuple-element.51), kind=kLoop, calls=%fused_computation | loop fusion | flops 4194304 | bytes 16777216 | tf_op jit(solution)/shard_map/transpose | solution.py:256
  296.8 8.3 %copy.14 = bf16[4,2,2,2,64,2048]{5,4,3,2,1,0:T(8,128)(2,1)} copy(bf16[4,2,2,2,64,2048]{5,4,0,2,1,3:T(8,128)(2,1)} %maximum_bitcast_fusion) | data formatting | bytes 16777216 | tf_op jit(solution)/shard_map/transpose | solution.py:256
  305.1 3.6 %all-to-all-done.1.refs_1_ = bf16[4,512,256]{2,1,0:T(8,128)(2,1)S(1)} async-done(((bf16[4,512,256]{2,1,0:T(8,128)(2,1)}), bf16[4,512,256]{2,1,0:T(8,128)(2,1)S(1)}, u32[]{:S(2)}, u32[]{:S(2)}) %all-to-all-start.1) | async-done | bytes 1048608 | tf_op jit(solution)/shard_map/all_to_all | solution.py:290
  308.7 1.0 copy-done.2
  309.7 1.2 copy-done.3
  310.9 8.2 %mix.1 = bf16[512,2048]{1,0:T(8,128)(2,1)} custom-call(bf16[4,512,256]{2,1,0:T(8,128)(2,1)S(1)} %all-to-all-done.refs_0_, bf16[4,512,256]{2,1,0:T(8,128)(2,1)S(1)} %copy-done.3, bf16[2048,2048]{1,0:T(8,128)(2,1)} %bitcast.35), custom_call_target="tpu_custom_call" | custom-call | tf_op jit(solution)/shard_map/mix/pallas_call | solution.py:219
  (66 shorter events, 0.4 us)
Async XLA Ops:
  6.5 3.4 %copy-start = (bf16[512,2048]{1,0:T(8,128)(2,1)S(1)}, bf16[512,2048]{1,0:T(8,128)(2,1)}, u32[]{:S(2)}) copy-start(bf16[512,2048]{1,0:T(8,128)(2,1)} %param.15) | copy-start | bytes 6291460
  6.5 115.7 %all-gather.11.cloned.1.call-start = ((), (), s32[]{:S(2)}) async-start(), calls=%async_computation.3 | async-start | bytes 5242880 | tf_op jit(solution)/shard_map/all_gather | solution.py:269
  9.9 179.1 %all-gather.9.cloned.1.call-start = ((), (), s32[]{:S(2)}) async-start(), calls=%async_computation.2 | async-start | bytes 5242880 | tf_op jit(solution)/shard_map/all_gather | solution.py:269
  9.9 12.0 %collective-permute-start.2 = (bf16[64,2048]{1,0:T(8,128)(2,1)S(1)}, bf16[64,2048]{1,0:T(8,128)(2,1)S(1)}, u32[]{:S(2)}, u32[]{:S(2)}) collective-permute-start(bf16[64,2048]{1,0:T(8,128)(2,1)S(1)} %constant_dynamic-slice_fusion.4), channel_id=1, source_target_pairs={{0,3},{1,0},{2,1},{3,2},{4,7},{5,4},{6,5},{7,6},{8,11},{9,8},{10,9... | collective-permute-start | bytes 786440 | tf_op jit(solution)/shard_map/ppermute | solution.py:239
  15.1 39.2 %collective-permute-start.1 = (bf16[64,2048]{1,0:T(8,128)(2,1)S(1)}, bf16[64,2048]{1,0:T(8,128)(2,1)S(1)}, u32[]{:S(2)}, u32[]{:S(2)}) collective-permute-start(bf16[64,2048]{1,0:T(8,128)(2,1)S(1)} %constant_dynamic-slice_fusion.4), channel_id=1, source_target_pairs={{0,2},{1,3},{2,0},{3,1},{4,6},{5,7},{6,4},{7,5},{8,10},{9,11},{10,... | collective-permute-start | bytes 786440 | tf_op jit(solution)/shard_map/ppermute | solution.py:239
  15.1 39.2 %collective-permute-start = (bf16[64,2048]{1,0:T(8,128)(2,1)S(1)}, bf16[64,2048]{1,0:T(8,128)(2,1)S(1)}, u32[]{:S(2)}, u32[]{:S(2)}) collective-permute-start(bf16[64,2048]{1,0:T(8,128)(2,1)S(1)} %constant_dynamic-slice_fusion.4), channel_id=1, source_target_pairs={{0,1},{1,2},{2,3},{3,0},{4,5},{5,6},{6,7},{7,4},{8,9},{9,10},{10,1... | collective-permute-start | bytes 786440 | tf_op jit(solution)/shard_map/ppermute | solution.py:239
  54.7 19.0 %collective-permute-start.3 = (bf16[4,64,2048]{2,1,0:T(8,128)(2,1)S(1)}, bf16[4,64,2048]{2,1,0:T(8,128)(2,1)S(1)}, u32[]{:S(2)}, u32[]{:S(2)}) collective-permute-start(bf16[4,64,2048]{2,1,0:T(8,128)(2,1)S(1)} %pad_maximum_fusion.3), channel_id=1, source_target_pairs={{0,8},{4,12},{8,0},{12,4},{16,24},{20,28},{24,16},{28,20},{1,9},{5... | collective-permute-start | bytes 3145736 | tf_op jit(solution)/shard_map/ppermute | solution.py:252
  56.2 185.6 %all-gather.13.cloned.1.call-start = ((), (), s32[]{:S(2)}) async-start(), calls=%async_computation.4 | async-start | bytes 1179648 | tf_op jit(solution)/shard_map/all_gather | solution.py:279
  73.8 1.0 copy-start.31
  73.8 1.3 copy-start.32
  73.8 2.9 copy-start.33
  75.2 5.2 %copy-start.35 = (f32[4]{0:T(128)S(1)}, f32[4]{0:T(128)}, u32[]{:S(2)}) copy-start(f32[4]{0:T(128)} %param.13) | copy-start | bytes 52
  75.2 40.7 %collective-permute-start.4 = (bf16[2,4,64,2048]{3,2,1,0:T(8,128)(2,1)S(1)}, bf16[2,4,64,2048]{3,2,1,0:T(8,128)(2,1)}, u32[]{:S(2)}, u32[]{:S(2)}) collective-permute-start(bf16[2,4,64,2048]{3,2,1,0:T(8,128)(2,1)S(1)} %pad_maximum_fusion.1), channel_id=1, source_target_pairs={{0,16},{4,20},{8,24},{12,28},{16,0},{20,4},{24,8},{28,12},{1,17},{... | collective-permute-start | bytes 6291464 | tf_op jit(solution)/shard_map/ppermute | solution.py:252
  78.2 44.1 %copy-start.16 = (bf16[2048,128]{1,0:T(8,128)(2,1)}, bf16[2048,128]{1,0:T(8,128)(2,1)S(1)}, u32[]{:S(2)}) copy-start(bf16[2048,128]{1,0:T(8,128)(2,1)S(1)} %pad.18.wb) | copy-start | bytes 1572868
  118.5 1.3 copy-start.30
  118.6 3.7 %copy-start.29 = (bf16[1,2,4,64,2048]{4,3,2,1,0:T(8,128)(2,1)}, bf16[1,2,4,64,2048]{4,3,2,1,0:T(8,128)(2,1)S(1)}, u32[]{:S(2)}) copy-start(bf16[1,2,4,64,2048]{4,3,2,1,0:T(8,128)(2,1)S(1)} %get-tuple-element.53) | copy-start | bytes 6291460
  122.3 161.2 %collective-permute-start.5 = (bf16[2,2,4,64,2048]{4,3,2,1,0:T(8,128)(2,1)}, bf16[2,2,4,64,2048]{4,3,2,1,0:T(8,128)(2,1)}, u32[]{:S(2)}, u32[]{:S(2)}) collective-permute-start(bf16[2,2,4,64,2048]{4,3,2,1,0:T(8,128)(2,1)} %pad_maximum_fusion), channel_id=1, source_target_pairs={{0,4},{4,0},{8,12},{12,8},{16,20},{20,16},{24,28},{28,24},{1,5},{5... | collective-permute-start | bytes 12582920 | tf_op jit(solution)/shard_map/ppermute | solution.py:252
  122.3 1.6 copy-start.26
  123.9 19.6 %copy-start.14 = (bf16[2048,128]{1,0:T(8,128)(2,1)S(1)}, bf16[2048,128]{1,0:T(8,128)(2,1)}, u32[]{:S(2)}) copy-start(bf16[2048,128]{1,0:T(8,128)(2,1)} %pad.20.wb) | copy-start | bytes 1572868
  142.6 0.8 copy-start.20
  162.1 1.0 copy-start.6
  163.1 0.8 copy-start.18
  189.0 1.0 copy-start.17
  190.0 1.6 copy-start.27
  210.3 1.0 copy-start.8
  211.3 0.8 copy-start.22
  214.1 1.3 copy-start.4
  215.4 48.6 %all-gather.15.cloned.1.call-start = ((), (), s32[]{:S(2)}) async-start(), calls=%async_computation.5 | async-start | bytes 1179648 | tf_op jit(solution)/shard_map/all_gather | solution.py:279
  215.5 1.0 copy-start.15
  216.5 1.6 copy-start.28
  236.8 1.0 copy-start.10
  237.8 0.8 copy-start.24
  238.6 3.3 %copy-start.34 = (f32[512]{0:T(512)S(1)}, f32[512]{0:T(512)}, u32[]{:S(2)}) copy-start(f32[512]{0:T(512)} %param.14) | copy-start | bytes 6148
  238.6 3.3 %copy-start.9 = (f32[4,256,256]{2,1,0:T(8,128)S(1)}, f32[4,256,256]{2,1,0:T(8,128)}, u32[]{:S(2)}) copy-start(f32[4,256,256]{2,1,0:T(8,128)} %copy-done.8) | copy-start | bytes 3145732
  240.5 1.3 copy-start.5
  241.9 1.2 copy-start.12
  243.1 1.0 copy-start.21
  244.2 1.0 copy-start.23
  250.1 14.0 %copy-start.7 = (f32[4,256,256]{2,1,0:T(8,128)S(1)}, f32[4,256,256]{2,1,0:T(8,128)}, u32[]{:S(2)}) copy-start(f32[4,256,256]{2,1,0:T(8,128)} %copy-done.6) | copy-start | bytes 3145732
  250.1 14.0 %copy-start.11 = (f32[4,256,256]{2,1,0:T(8,128)S(1)}, f32[4,256,256]{2,1,0:T(8,128)}, u32[]{:S(2)}) copy-start(f32[4,256,256]{2,1,0:T(8,128)} %copy-done.10) | copy-start | bytes 3145732
  250.1 29.8 %all-to-all-start = ((bf16[4,512,256]{2,1,0:T(8,128)(2,1)}), bf16[4,512,256]{2,1,0:T(8,128)(2,1)S(1)}, u32[]{:S(2)}, u32[]{:S(2)}) async-start(bf16[4,512,256]{2,1,0:T(8,128)(2,1)} %emit.2), calls=%async_computation | async-start | bytes 2097152 | tf_op jit(solution)/shard_map/all_to_all | solution.py:290
  264.0 1.2 copy-start.13
  265.3 1.0 copy-start.19
  266.3 1.0 copy-start.25
  279.9 28.8 %all-to-all-start.1 = ((bf16[4,512,256]{2,1,0:T(8,128)(2,1)}), bf16[4,512,256]{2,1,0:T(8,128)(2,1)S(1)}, u32[]{:S(2)}, u32[]{:S(2)}) async-start(bf16[4,512,256]{2,1,0:T(8,128)(2,1)} %emit.3), calls=%async_computation.1 | async-start | bytes 2097152 | tf_op jit(solution)/shard_map/all_to_all | solution.py:290
  308.7 1.0 copy-start.2
  309.7 1.2 copy-start.3
  310.9 8.2 %copy-start.1 = (bf16[512,2048]{1,0:T(8,128)(2,1)S(1)}, bf16[512,2048]{1,0:T(8,128)(2,1)}, u32[]{:S(2)}) copy-start(bf16[512,2048]{1,0:T(8,128)(2,1)} %param.15) | copy-start | bytes 6291460
Sparse Core Ops, SparseCore 0:
  10.0 95.4 all-gather.10
  107.1 81.8 all-gather.8
  215.5 22.0 all-gather.12
  242.0 22.0 all-gather.14

commit v3 on v2

--- a/solution.py
+++ b/solution.py
@@ -7,8 +7,8 @@
 from jax.experimental.pallas import tpu as pltpu
 from jax.sharding import PartitionSpec as P
 
-CHUNK = 256
 LANES = 128
+CHUNKS = (256, 128, 128)
 VMEM = 48 * 2**20
 half = jnp.bfloat16
 single = jnp.float32
@@ -35,6 +35,7 @@
 def chunk_kernel(heads, tok, wq, wk, wv, wb, gain, reads_ref, outs_ref, trans_ref):
     width = wq.shape[1] // heads
     x = tok[0]
+    size = x.shape[0]
     each = range(heads)
 
     def project(w):
@@ -44,8 +45,8 @@
     k = [unit(a) for a in project(wk)]
     beta = gain[...] * jax.nn.sigmoid(jnp.dot(x, wb[...], preferred_element_type=single))
     rates = [beta[:, h : h + 1] for h in each]
-    row = lax.broadcasted_iota(jnp.int32, (CHUNK, CHUNK), 0)
-    col = lax.broadcasted_iota(jnp.int32, (CHUNK, CHUNK), 1)
+    row = lax.broadcasted_iota(jnp.int32, (size, size), 0)
+    col = lax.broadcasted_iota(jnp.int32, (size, size), 1)
     near = (row // 16) == (col // 16)
     mid = (row // 64) == (col // 64)
     below = row > col
@@ -78,7 +79,7 @@
 
 
 def chunk_terms(tokens, wq, wk, wv, wb, gain, heads, group):
-    chunks, _, depth = tokens.shape
+    chunks, size, depth = tokens.shape
     width = wq.shape[1] // wb.shape[1]
     per = heads * width
     gain = jnp.pad(gain[group * heads : (group + 1) * heads], (0, LANES - heads))
@@ -92,26 +93,26 @@
     return pl.pallas_call(
         functools.partial(chunk_kernel, heads),
         grid=(chunks,),
-        in_specs=[pl.BlockSpec((1, CHUNK, depth), lambda i: (i, 0, 0))]
+        in_specs=[pl.BlockSpec((1, size, depth), lambda i: (i, 0, 0))]
         + [
             pl.BlockSpec((depth, per), lambda i: (0, group), pipeline_mode=pl.Buffered(1))
             for _ in range(3)
         ]
         + [once(w.shape) for w in (wb, gain)],
         out_specs=[
-            pl.BlockSpec((1, CHUNK, per), lambda i: (i, 0, 0)),
-            pl.BlockSpec((1, CHUNK, per), lambda i: (i, 0, 0)),
+            pl.BlockSpec((1, size, per), lambda i: (i, 0, 0)),
+            pl.BlockSpec((1, size, per), lambda i: (i, 0, 0)),
             pl.BlockSpec((1, heads, width, 2 * width), lambda i: (i, 0, 0, 0)),
         ],
         out_shape=[
-            jax.ShapeDtypeStruct((chunks, CHUNK, per), half),
-            jax.ShapeDtypeStruct((chunks, CHUNK, per), single),
+            jax.ShapeDtypeStruct((chunks, size, per), half),
+            jax.ShapeDtypeStruct((chunks, size, per), single),
             jax.ShapeDtypeStruct((chunks, heads, width, 2 * width), single),
         ],
         compiler_params=pltpu.CompilerParams(vmem_limit_bytes=VMEM),
         cost_estimate=pl.CostEstimate(
-            flops=2 * chunks * CHUNK * (depth * 3 * per + heads * 18 * CHUNK * CHUNK),
-            bytes_accessed=2 * depth * 3 * per + chunks * CHUNK * (2 * depth + 8 * per),
+            flops=2 * chunks * size * (depth * 3 * per + heads * 18 * size * size),
+            bytes_accessed=2 * depth * 3 * per + chunks * size * (2 * depth + 8 * per),
             transcendentals=0,
         ),
         name="chunk_terms",
@@ -165,14 +166,16 @@
 
         lax.fori_loop(0, place_ref[0], one, 0)
 
+    first = 0
     for part in range(parts):
+        rows = slice(first, first + reads[part].shape[1])
+        first = rows.stop
         for h in range(heads):
             here = slice(h * width, (h + 1) * width)
             pair = starts_ref[0, part, h]
             state = mm(pair[:, :width], entry[h]) + pair[:, width:]
             o = mm(reads[part][0, :, here], state) + outs[part][0, :, here]
             scale = lax.rsqrt(jnp.mean(o * o, -1, keepdims=True) + 1e-05)
-            rows = slice(part * CHUNK, (part + 1) * CHUNK)
             result[0, rows, here] = (o * scale * gain[:, here]).astype(half)
 
 
@@ -180,7 +183,8 @@
     parts = len(reads)
     chunks, _, per = reads[0].shape
     _, _, heads, width, wide = starts.shape
-    rows = pl.BlockSpec((1, CHUNK, per), lambda i: (i, 0, 0))
+    rows = [pl.BlockSpec((1, a.shape[1], per), lambda i: (i, 0, 0)) for a in reads]
+    count = sum(a.shape[1] for a in reads)
     return pl.pallas_call(
         functools.partial(emit_kernel, parts),
         grid=(chunks,),
@@ -192,9 +196,9 @@
             pl.BlockSpec((1, parts, heads, width, wide), lambda i: (i, 0, 0, 0, 0)),
             pl.BlockSpec((1, per), lambda i: (0, 0)),
         ]
-        + [rows] * (2 * parts),
-        out_specs=pl.BlockSpec((1, parts * CHUNK, per), lambda i: (i, 0, 0)),
-        out_shape=jax.ShapeDtypeStruct((chunks, parts * CHUNK, per), half),
+        + rows * 2,
+        out_specs=pl.BlockSpec((1, count, per), lambda i: (i, 0, 0)),
+        out_shape=jax.ShapeDtypeStruct((chunks, count, per), half),
         scratch_shapes=[pltpu.VMEM((heads, width, width), single)],
         compiler_params=pltpu.CompilerParams(vmem_limit_bytes=VMEM),
         name="emit",
@@ -261,19 +265,21 @@
     per = w_query.shape[1]
     heads = w_beta.shape[1]
     place = lax.axis_index("seq")
-    parts = tokens.shape[0] // CHUNK
-    groups = 2
+    groups = 1
     few = heads // groups
     w_whole = whole_weight(w_out, seqs, owners)
+    ends = [sum(CHUNKS[: i + 1]) for i in range(len(CHUNKS))]
     pieces = [
-        lax.all_gather(tokens[part * CHUNK : (part + 1) * CHUNK], "head", axis=0)
-        for part in range(parts)
+        lax.all_gather(tokens[end - size : end], "head", axis=0)
+        for size, end in zip(CHUNKS, ends)
     ]
     weights = (w_query, w_key, w_value, w_beta, beta_gain)
     done = []
     for a in pieces:
         if done:
             a, done[-1] = lax.optimization_barrier((a, done[-1]))
+        if len(done) == 1:
+            a, w_whole = lax.optimization_barrier((a, w_whole))
         done.append([chunk_terms(a, *weights, few, g) for g in range(groups)])
     pairs = [fold([a[g][2] for a in done]) for g in range(groups)]
     everyone = [lax.all_gather(last, "seq", axis=0) for _, last in pairs]

time: 327 us -> 348 us (1.064)
  blocking collectives: 0 us -> 53.4 us
  local copies, waits for them, and re-layouts: 42.4 us -> 27.1 us
  Pallas kernels: 96.6 us -> 86.3 us
  starting transfers between devices: 16.5 us -> 11.8 us
  waiting for transfers between devices: 138 us -> 134 us
    all_to_all x0 -> x1, blocking collectives: none -> 53.4 us  [body(): lax.all_to_all(normed, 'head', split_axis=0, concat_axis=0, tiled=True)]
    all_gather x2 -> x1, waiting for transfers between devices: 10.3 us -> 39.7 us  [body(): everyone = [lax.all_gather(last, 'seq', axis=0) for _, last in pairs]]
    unnamed x74 -> x47, local copies, waits for them, and re-layouts: 28.3 us -> 14.1 us
    ppermute x3, waiting for transfers between devices: 38.2 us -> 25.5 us  [whole_weight(): turned.append(lax.ppermute(mine, 'head', pairs))]
    all_gather x2 -> x3, waiting for transfers between devices: 25.1 us -> 12.7 us  [body(): lax.all_gather(tokens[end - size:end], 'head', axis=0)]
    pallas_call x4 -> x3, Pallas kernels: 74.8 us -> 63.3 us  [chunk_terms(): pl.pallas_call(functools.partial(chunk_kernel, heads), grid=(chunks,), in...]
    all_to_all x2 -> x0, waiting for transfers between devices: 11.3 us -> none  [body(): lax.all_to_all(normed, 'head', split_axis=0, concat_axis=0, tiled=True)]
    all_to_all x2 -> x0, starting transfers between devices: 7.16 us -> none  [body(): lax.all_to_all(normed, 'head', split_axis=0, concat_axis=0, tiled=True)]
  transfers between devices with their start and end apart: 12 -> 10, of which waited for: 8 -> 6; matrix products, arithmetic and copies ran while one was open for 10% -> 9% of each run, Pallas kernels for 27% -> 13%
where the time goes in v3:
time: 348 us
  waiting for transfers between devices  134 us (39%)
  Pallas kernels  86.3 us (25%)
  blocking collectives  53.4 us (15%)
  local copies, waits for them, and re-layouts  27.1 us (8%)
  other arithmetic  21.2 us (6%)
  between operations  13.3 us (4%)
  starting transfers between devices  11.8 us (3%)
    pallas_call x3, Pallas kernels, chunk_terms(): pl.pallas_call(functools.partial(chunk_kernel, heads), grid=(chunks,), in...  63.3 us
    ppermute x3, waiting for transfers between devices, whole_weight(): other = lax.ppermute(held, 'seq', pairs)  56.5 us
    all_to_all x1, blocking collectives, body(): lax.all_to_all(normed, 'head', split_axis=0, concat_axis=0, tiled=True)  53.4 us
    all_gather x1, waiting for transfers between devices, body(): everyone = [lax.all_gather(last, 'seq', axis=0) for _, last in pairs]  39.7 us
    ppermute x3, waiting for transfers between devices, whole_weight(): turned.append(lax.ppermute(mine, 'head', pairs))  25.5 us
    unnamed x47, local copies, waits for them, and re-layouts  14.1 us
    another operation x5, other arithmetic, whole_weight(): jnp.stack([jnp.where(upper, other, held), jnp.where(upper, held, other)])  13 us
    all_gather x3, waiting for transfers between devices, body(): lax.all_gather(tokens[end - size:end], 'head', axis=0)  12.7 us
  transfers between devices with their start and end apart: 10, of which 6 were waited for; matrix products, arithmetic and copies ran while one was open for 9% of the time, Pallas kernels for 13%

profile of v3, /device:TPU:0, one launch (start us, length us, event | category | flops | bytes accessed | tf_op | source)
XLA Modules:
  0.0 347.6 jit_solution(7984154436661812597)
XLA Ops:
  6.5 0.0 copy-start
  6.5 2.5 slice.10
  9.0 0.0 all-gather.11.cloned.1.call-update
  9.1 0.0 all-gather.9.cloned.1.call-start
  9.2 4.1 %collective-permute-start.1 = (bf16[64,2048]{1,0:T(8,128)(2,1)S(1)}, bf16[64,2048]{1,0:T(8,128)(2,1)S(1)}, u32[]{:S(2)}, u32[]{:S(2)}) collective-permute-start(bf16[64,2048]{1,0:T(8,128)(2,1)S(1)} %constant_dynamic-slice_fusion.4), channel_id=1, source_target_pairs={{0,2},{1,3},{2,0},{3,1},{4,6},{5,7},{6,4},{7,5},{8,10},{9,11},{10,... | collective-permute-start | bytes 786440 | tf_op jit(solution)/shard_map/ppermute | solution.py:243
  13.3 1.6 collective-permute-start
  14.8 2.2 collective-permute-start.2
  17.1 25.5 %collective-permute-done.1 = bf16[64,2048]{1,0:T(8,128)(2,1)S(1)} collective-permute-done((bf16[64,2048]{1,0:T(8,128)(2,1)S(1)}, bf16[64,2048]{1,0:T(8,128)(2,1)S(1)}, u32[]{:S(2)}, u32[]{:S(2)}) %collective-permute-start.1) | collective-permute-done | bytes 262176 | tf_op jit(solution)/shard_map/ppermute | solution.py:243
  42.6 0.0 collective-permute-done
  42.6 0.0 collective-permute-done.2
  42.6 0.1 pad_maximum_fusion.2
  42.7 0.1 constant_dynamic-slice_fusion.3
  42.8 0.1 pad_maximum_fusion.3
  43.0 2.2 collective-permute-start.3
  45.2 17.6 %collective-permute-done.3 = bf16[4,64,2048]{2,1,0:T(8,128)(2,1)} collective-permute-done((bf16[4,64,2048]{2,1,0:T(8,128)(2,1)S(1)}, bf16[4,64,2048]{2,1,0:T(8,128)(2,1)}, u32[]{:S(2)}, u32[]{:S(2)}) %collective-permute-start.3) | collective-permute-done | bytes 1048608 | tf_op jit(solution)/shard_map/ppermute | solution.py:256
  62.8 1.4 select_bitcast_fusion.5
  64.2 0.0 copy-start.20
  64.2 1.5 pad_maximum_fusion.1
  65.7 1.3 collective-permute-start.4
  67.1 0.0 copy-done.20
  67.1 1.1 fusion
  68.1 0.0 all-gather.9.cloned.1.call-update
  68.2 0.0 all-gather.13.cloned.1.call-start
  68.2 38.9 %collective-permute-done.4 = bf16[2,4,64,2048]{3,2,1,0:T(8,128)(2,1)} collective-permute-done((bf16[2,4,64,2048]{3,2,1,0:T(8,128)(2,1)}, bf16[2,4,64,2048]{3,2,1,0:T(8,128)(2,1)}, u32[]{:S(2)}, u32[]{:S(2)}) %collective-permute-start.4) | collective-permute-done | bytes 2097184 | tf_op jit(solution)/shard_map/ppermute | solution.py:256
  107.1 1.9 select_bitcast_fusion.3
  109.0 0.0 copy-start.18
  109.0 0.0 copy-start.19
  109.0 1.3 copy-done.18
  110.3 2.4 pad_maximum_fusion
  112.7 0.0 collective-permute-start.5
  112.7 0.0 all-gather.13.cloned.1.call-update
  112.7 0.2 all-gather.15.cloned.1.call-start
  113.0 0.3 copy.11
  113.3 0.9 pad.12.wb
  114.2 1.1 copy-done.10
  115.3 26.2 %chunk_terms.3 = (bf16[4,256,512]{2,1,0:T(8,128)(2,1)S(1)}, f32[4,256,512]{2,1,0:T(8,128)S(1)}, f32[4,4,128,256]{3,2,1,0:T(8,128)S(1)}) custom-call(bf16[4,256,2048]{2,1,0:T(8,128)(2,1)} %bitcast.34, bf16[2048,512]{1,0:T(8,128)(2,1)} %wq.5, bf16[2048,512]{1,0:T(8,128)(2,1)} %wk.5, bf16[2048,512]{1,0:T(8,128)(2,1)} %wv.5, bf16[2048,128]{1,0:T(8,128)(2,1)S(1)} %copy-done.10, ...), custom_call_target="tpu_custom_call" | custom-call | flops 16106127360 | bytes 14680064 | tf_op jit(solution)/shard_map/chunk_terms/pallas_call | solution.py:93
  141.5 0.0 copy-start.5
  141.5 1.3 copy-done.5
  142.8 10.3 %all-gather.9.cloned.1.call-done = bf16[512,2048]{1,0:T(8,128)(2,1)} async-done(((bf16[128,2048]{1,0:T(8,128)(2,1)}), bf16[512,2048]{1,0:T(8,128)(2,1)}) %all-gather.9.cloned.1.call-update) | async-done | bytes 2097168 | tf_op jit(solution)/shard_map/all_gather | solution.py:273
  153.1 0.0 collective-permute-done.5
  153.1 5.8 %select_bitcast_fusion.1 = (bf16[1,2,2,4,64,2048]{5,4,3,2,1,0:T(8,128)(2,1)}, bf16[1,2,2,4,64,2048]{5,4,3,2,1,0:T(8,128)(2,1)}) fusion(bf16[2,2,4,64,2048]{4,3,2,1,0:T(8,128)(2,1)} %collective-permute-done.5, pred[]{:T(512)S(6)} %eq.14, bf16[1,2,4,64,2048]{4,3,2,1,0:T(8,128)(2,1)} %copy-done.19, bf16[1,2,4,64,2048]{4,3,2,1,0:T(8,128)(2,1)} %copy-done.18), kind=kLoop, calls=%fused_computation.3 | loop fusion | flops 6291456 | bytes 16777216 | tf_op jit(solution)/shard_map/stack | solution.py:258
  158.9 7.9 %maximum_bitcast_fusion = bf16[4,2,2,2,64,2048]{5,4,0,2,1,3:T(8,128)(2,1)} fusion(bf16[1,2,2,4,64,2048]{5,4,3,2,1,0:T(8,128)(2,1)} %get-tuple-element.48, bf16[1,2,2,4,64,2048]{5,4,3,2,1,0:T(8,128)(2,1)} %get-tuple-element.47), kind=kLoop, calls=%fused_computation | loop fusion | flops 4194304 | bytes 16777216 | tf_op jit(solution)/shard_map/transpose | solution.py:260
  166.9 8.4 %copy.12 = bf16[4,2,2,2,64,2048]{5,4,3,2,1,0:T(8,128)(2,1)} copy(bf16[4,2,2,2,64,2048]{5,4,0,2,1,3:T(8,128)(2,1)} %maximum_bitcast_fusion) | data formatting | bytes 16777216 | tf_op jit(solution)/shard_map/transpose | solution.py:260
  175.3 18.5 %chunk_terms.4 = (bf16[4,128,512]{2,1,0:T(8,128)(2,1)S(1)}, f32[4,128,512]{2,1,0:T(8,128)S(1)}, f32[4,4,128,256]{3,2,1,0:T(8,128)S(1)}) custom-call(bf16[4,128,2048]{2,1,0:T(8,128)(2,1)} %bitcast.35, bf16[2048,512]{1,0:T(8,128)(2,1)} %wq.5, bf16[2048,512]{1,0:T(8,128)(2,1)} %wk.5, bf16[2048,512]{1,0:T(8,128)(2,1)} %wv.5, bf16[2048,128]{1,0:T(8,128)(2,1)S(1)} %copy-done.11, ...), custom_call_target="tpu_custom_call" | custom-call | flops 4429185024 | bytes 10485760 | tf_op jit(solution)/shard_map/chunk_terms/pallas_call | solution.py:93
  193.8 0.0 copy-start.2
  193.8 1.3 copy-done.2
  195.1 1.0 copy-done.6
  196.1 0.8 copy-done.13
  196.9 2.4 all-gather.13.cloned.1.call-done
  199.4 1.0 copy-done.12
  200.4 18.6 %chunk_terms.5 = (bf16[4,128,512]{2,1,0:T(8,128)(2,1)S(1)}, f32[4,128,512]{2,1,0:T(8,128)S(1)}, f32[4,4,128,256]{3,2,1,0:T(8,128)S(1)}) custom-call(bf16[4,128,2048]{2,1,0:T(8,128)(2,1)} %bitcast.36, bf16[2048,512]{1,0:T(8,128)(2,1)} %wq.5, bf16[2048,512]{1,0:T(8,128)(2,1)} %wk.5, bf16[2048,512]{1,0:T(8,128)(2,1)} %wv.5, bf16[2048,128]{1,0:T(8,128)(2,1)S(1)} %copy-done.12, ...), custom_call_target="tpu_custom_call" | custom-call | flops 4429185024 | bytes 10485760 | tf_op jit(solution)/shard_map/chunk_terms/pallas_call | solution.py:93
  219.0 0.0 copy-start.4
  219.0 1.3 copy-done.4
  220.3 6.9 %fold.1 = (f32[4,3,4,128,256]{4,3,2,1,0:T(8,128)}, bf16[4,128,256]{2,1,0:T(8,128)(2,1)}) custom-call(f32[4,4,128,256]{3,2,1,0:T(8,128)S(1)} %get-tuple-element.29.refs_0_, f32[4,4,128,256]{3,2,1,0:T(8,128)S(1)} %copy-done.3, f32[4,4,128,256]{3,2,1,0:T(8,128)} %copy-done.4), custom_call_target="tpu_custom_call" | custom-call | tf_op jit(solution)/shard_map/fold/pallas_call | solution.py:142
  227.2 0.0 copy-done.15
  227.2 0.0 all-gather.15.cloned.1.call-update
  227.2 39.7 %all-gather.15.cloned.1.call-done = bf16[32,128,256]{2,1,0:T(8,128)(2,1)} async-done(((bf16[4,128,256]{2,1,0:T(8,128)(2,1)}), bf16[32,128,256]{2,1,0:T(8,128)(2,1)}) %all-gather.15.cloned.1.call-update) | async-done | bytes 2097168 | tf_op jit(solution)/shard_map/all_gather | solution.py:285
  267.0 1.2 copy-done.7
  268.2 1.2 copy-done.9
  269.4 1.0 copy-done.14
  270.5 1.0 copy-done.16
  271.5 8.0 %emit.1 = bf16[4,512,512]{2,1,0:T(8,128)(2,1)} custom-call(s32[1]{0:T(128)} %bitcast.place_ref, bf16[8,4,128,256]{3,2,1,0:T(8,128)(2,1)} %bitcast.30, f32[4,3,4,128,256]{4,3,2,1,0:T(8,128)} %get-tuple-element.39.starts_ref, f32[1,512]{1,0:T(1,128)S(1)} %bitcast.28, bf16[4,256,512]{2,1,0:T(8,128)(2,1)S(1)} %get-tuple-element.40.refs_0_, ...), custom_call_target="tpu_custom_call" | custom-call | tf_op jit(solution)/shard_map/emit/pallas_call | solution.py:188
  279.5 53.4 %all_to_all.5.refs_0_ = bf16[4,512,512]{2,1,0:T(8,128)(2,1)S(1)} all-to-all(bf16[4,512,512]{2,1,0:T(8,128)(2,1)} %emit.1), channel_id=1, replica_groups=mesh['seq'=8,'head'=4] {'head'}, dimensions={0} | all-to-all | bytes 4194304 | tf_op jit(solution)/shard_map/all_to_all | solution.py:296
  332.9 8.2 %mix.1 = bf16[512,2048]{1,0:T(8,128)(2,1)} custom-call(bf16[4,512,512]{2,1,0:T(8,128)(2,1)S(1)} %all_to_all.5.refs_0_, bf16[2048,2048]{1,0:T(8,128)(2,1)} %bitcast.29), custom_call_target="tpu_custom_call" | custom-call | tf_op jit(solution)/shard_map/mix/pallas_call | solution.py:223
  (30 shorter events, 0.1 us)
Async XLA Ops:
  6.5 2.6 copy-start
  6.5 107.7 %all-gather.11.cloned.1.call-start = ((), (), s32[]{:S(2)}) async-start(), calls=%async_computation.2 | async-start | bytes 5242880 | tf_op jit(solution)/shard_map/all_gather | solution.py:273
  9.1 144.0 %all-gather.9.cloned.1.call-start = ((), (), s32[]{:S(2)}) async-start(), calls=%async_computation.1 | async-start | bytes 2621440 | tf_op jit(solution)/shard_map/all_gather | solution.py:273
  9.2 33.4 %collective-permute-start.1 = (bf16[64,2048]{1,0:T(8,128)(2,1)S(1)}, bf16[64,2048]{1,0:T(8,128)(2,1)S(1)}, u32[]{:S(2)}, u32[]{:S(2)}) collective-permute-start(bf16[64,2048]{1,0:T(8,128)(2,1)S(1)} %constant_dynamic-slice_fusion.4), channel_id=1, source_target_pairs={{0,2},{1,3},{2,0},{3,1},{4,6},{5,7},{6,4},{7,5},{8,10},{9,11},{10,... | collective-permute-start | bytes 786440 | tf_op jit(solution)/shard_map/ppermute | solution.py:243
  13.3 29.3 %collective-permute-start = (bf16[64,2048]{1,0:T(8,128)(2,1)S(1)}, bf16[64,2048]{1,0:T(8,128)(2,1)S(1)}, u32[]{:S(2)}, u32[]{:S(2)}) collective-permute-start(bf16[64,2048]{1,0:T(8,128)(2,1)S(1)} %constant_dynamic-slice_fusion.4), channel_id=1, source_target_pairs={{0,1},{1,2},{2,3},{3,0},{4,5},{5,6},{6,7},{7,4},{8,9},{9,10},{10,1... | collective-permute-start | bytes 786440 | tf_op jit(solution)/shard_map/ppermute | solution.py:243
  14.8 27.8 %collective-permute-start.2 = (bf16[64,2048]{1,0:T(8,128)(2,1)S(1)}, bf16[64,2048]{1,0:T(8,128)(2,1)S(1)}, u32[]{:S(2)}, u32[]{:S(2)}) collective-permute-start(bf16[64,2048]{1,0:T(8,128)(2,1)S(1)} %constant_dynamic-slice_fusion.4), channel_id=1, source_target_pairs={{0,3},{1,0},{2,1},{3,2},{4,7},{5,4},{6,5},{7,6},{8,11},{9,8},{10,9... | collective-permute-start | bytes 786440 | tf_op jit(solution)/shard_map/ppermute | solution.py:243
  43.0 19.8 %collective-permute-start.3 = (bf16[4,64,2048]{2,1,0:T(8,128)(2,1)S(1)}, bf16[4,64,2048]{2,1,0:T(8,128)(2,1)}, u32[]{:S(2)}, u32[]{:S(2)}) collective-permute-start(bf16[4,64,2048]{2,1,0:T(8,128)(2,1)S(1)} %pad_maximum_fusion.3), channel_id=1, source_target_pairs={{0,8},{4,12},{8,0},{12,4},{16,24},{20,28},{24,16},{28,20},{1,9},{5... | collective-permute-start | bytes 3145736 | tf_op jit(solution)/shard_map/ppermute | solution.py:256
  64.2 2.8 copy-start.20
  65.7 41.4 %collective-permute-start.4 = (bf16[2,4,64,2048]{3,2,1,0:T(8,128)(2,1)}, bf16[2,4,64,2048]{3,2,1,0:T(8,128)(2,1)}, u32[]{:S(2)}, u32[]{:S(2)}) collective-permute-start(bf16[2,4,64,2048]{3,2,1,0:T(8,128)(2,1)} %pad_maximum_fusion.1), channel_id=1, source_target_pairs={{0,16},{4,20},{8,24},{12,28},{16,0},{20,4},{24,8},{28,12},{1,17},{... | collective-permute-start | bytes 6291464 | tf_op jit(solution)/shard_map/ppermute | solution.py:256
  68.2 131.2 %all-gather.13.cloned.1.call-start = ((), (), s32[]{:S(2)}) async-start(), calls=%async_computation.3 | async-start | bytes 2621440 | tf_op jit(solution)/shard_map/all_gather | solution.py:273
  109.0 1.3 copy-start.18
  109.0 3.7 %copy-start.19 = (bf16[1,2,4,64,2048]{4,3,2,1,0:T(8,128)(2,1)}, bf16[1,2,4,64,2048]{4,3,2,1,0:T(8,128)(2,1)S(1)}, u32[]{:S(2)}) copy-start(bf16[1,2,4,64,2048]{4,3,2,1,0:T(8,128)(2,1)S(1)} %get-tuple-element.50) | copy-start | bytes 6291460
  110.3 2.7 copy-start.22
  110.3 2.7 copy-start.21
  112.7 40.4 %collective-permute-start.5 = (bf16[2,2,4,64,2048]{4,3,2,1,0:T(8,128)(2,1)}, bf16[2,2,4,64,2048]{4,3,2,1,0:T(8,128)(2,1)}, u32[]{:S(2)}, u32[]{:S(2)}) collective-permute-start(bf16[2,2,4,64,2048]{4,3,2,1,0:T(8,128)(2,1)} %pad_maximum_fusion), channel_id=1, source_target_pairs={{0,4},{4,0},{8,12},{12,8},{16,20},{20,16},{24,28},{28,24},{1,5},{5... | collective-permute-start | bytes 12582920 | tf_op jit(solution)/shard_map/ppermute | solution.py:256
  112.7 154.2 %all-gather.15.cloned.1.call-start = ((), (), s32[]{:S(2)}) async-start(), calls=%async_computation.4 | async-start | bytes 2359296 | tf_op jit(solution)/shard_map/all_gather | solution.py:285
  114.2 1.1 copy-start.10
  141.5 1.4 copy-start.5
  166.9 8.4 %copy-start.11 = (bf16[2048,128]{1,0:T(8,128)(2,1)S(1)}, bf16[2048,128]{1,0:T(8,128)(2,1)}, u32[]{:S(2)}) copy-start(bf16[2048,128]{1,0:T(8,128)(2,1)} %pad.12.wb) | copy-start | bytes 1572868
  193.8 1.3 copy-start.2
  195.1 1.0 copy-start.6
  196.1 0.8 copy-start.13
  199.4 1.0 copy-start.12
  200.4 19.9 %copy-start.3 = (f32[4,4,128,256]{3,2,1,0:T(8,128)S(1)}, f32[4,4,128,256]{3,2,1,0:T(8,128)}, u32[]{:S(2)}) copy-start(f32[4,4,128,256]{3,2,1,0:T(8,128)} %copy-done.2) | copy-start | bytes 6291460
  219.0 1.3 copy-start.4
  220.3 6.9 %copy-start.8 = (f32[4,128,512]{2,1,0:T(8,128)}, f32[4,128,512]{2,1,0:T(8,128)S(1)}, u32[]{:S(2)}) copy-start(f32[4,128,512]{2,1,0:T(8,128)S(1)} %get-tuple-element.45.refs_5_) | copy-start | bytes 3145732
  220.3 6.9 %copy-start.15 = (bf16[4,128,512]{2,1,0:T(8,128)(2,1)}, bf16[4,128,512]{2,1,0:T(8,128)(2,1)S(1)}, u32[]{:S(2)}) copy-start(bf16[4,128,512]{2,1,0:T(8,128)(2,1)S(1)} %get-tuple-element.42.refs_2_) | copy-start | bytes 1572868
  220.3 46.6 %copy-start.17 = (f32[512]{0:T(512)S(1)}, f32[512]{0:T(512)}, u32[]{:S(2)}) copy-start(f32[512]{0:T(512)} %param.14) | copy-start | bytes 6148
  267.0 1.2 copy-start.7
  268.2 1.2 copy-start.9
  269.4 1.0 copy-start.14
  270.5 1.0 copy-start.16
  332.9 8.2 %copy-start.1 = (bf16[512,2048]{1,0:T(8,128)(2,1)S(1)}, bf16[512,2048]{1,0:T(8,128)(2,1)}, u32[]{:S(2)}) copy-start(bf16[512,2048]{1,0:T(8,128)(2,1)} %param.15) | copy-start | bytes 6291460
Sparse Core Ops, SparseCore 0:
  9.2 95.2 all-gather.10
  106.0 47.0 all-gather.8
  154.7 44.6 all-gather.12
  227.3 39.5 all-gather.14

commit v4 on v3

--- a/solution.py
+++ b/solution.py
@@ -8,7 +8,7 @@
 from jax.sharding import PartitionSpec as P
 
 LANES = 128
-CHUNKS = (256, 128, 128)
+CHUNKS = (256, 256)
 VMEM = 48 * 2**20
 half = jnp.bfloat16
 single = jnp.float32
@@ -128,7 +128,7 @@
     for place in range(chunks):
         for part in range(parts):
             for h in range(heads):
-                starts_ref[place, part, h] = state[h]
+                starts_ref[part, place, h] = state[h]
                 step = trans[part][place, h]
                 moved = state[h] - mm(step[:, :width], state[h])
                 state[h] = moved + jnp.where(col < width, 0.0, step)
@@ -142,7 +142,7 @@
     return pl.pallas_call(
         functools.partial(fold_kernel, parts),
         out_shape=[
-            jax.ShapeDtypeStruct((chunks, parts, heads, width, wide), single),
+            jax.ShapeDtypeStruct((parts, chunks, heads, width, wide), single),
             jax.ShapeDtypeStruct((heads, width, wide), half),
         ],
         compiler_params=pltpu.CompilerParams(vmem_limit_bytes=VMEM),
@@ -172,14 +172,14 @@
         first = rows.stop
         for h in range(heads):
             here = slice(h * width, (h + 1) * width)
-            pair = starts_ref[0, part, h]
+            pair = starts_ref[0, 0, h]
             state = mm(pair[:, :width], entry[h]) + pair[:, width:]
             o = mm(reads[part][0, :, here], state) + outs[part][0, :, here]
             scale = lax.rsqrt(jnp.mean(o * o, -1, keepdims=True) + 1e-05)
             result[0, rows, here] = (o * scale * gain[:, here]).astype(half)
 
 
-def emit(place, everyone, starts, gain, reads, outs):
+def emit(part, place, everyone, starts, gain, reads, outs):
     parts = len(reads)
     chunks, _, per = reads[0].shape
     _, _, heads, width, wide = starts.shape
@@ -193,7 +193,7 @@
             pl.BlockSpec(
                 everyone.shape, lambda i: (0, 0, 0, 0), pipeline_mode=pl.Buffered(1)
             ),
-            pl.BlockSpec((1, parts, heads, width, wide), lambda i: (i, 0, 0, 0, 0)),
+            pl.BlockSpec((1, 1, heads, width, wide), lambda i: (part, i, 0, 0, 0)),
             pl.BlockSpec((1, per), lambda i: (0, 0)),
         ]
         + rows * 2,
@@ -205,20 +205,21 @@
     )(place, everyone, starts, gain, *reads, *outs)
 
 
-def mix_kernel(groups, *refs):
-    rows, (w, out) = refs[:groups], refs[groups:]
-    owners, _, width = rows[0].shape
-    total = 0.0
-    for owner in range(owners):
-        for g in range(groups):
-            first = (owner * groups + g) * width
-            total += mm(rows[g][owner], w[first : first + width, :])
-    out[...] = total.astype(half)
+def mix_kernel(parts, *refs):
+    rows, (w, out) = refs[:parts], refs[parts:]
+    first = 0
+    for part in rows:
+        owners, count, width = part.shape
+        total = mm(part[0], w[:width, :])
+        for owner in range(1, owners):
+            total += mm(part[owner], w[owner * width : (owner + 1) * width, :])
+        out[first : first + count, :] = total.astype(half)
+        first += count
 
 
 def mix(rows, w_whole):
     depth, columns = w_whole.shape
-    count = rows[0].shape[1]
+    count = sum(a.shape[1] for a in rows)
     tile = 512
     return pl.pallas_call(
         functools.partial(mix_kernel, len(rows)),
@@ -265,8 +266,6 @@
     per = w_query.shape[1]
     heads = w_beta.shape[1]
     place = lax.axis_index("seq")
-    groups = 1
-    few = heads // groups
     w_whole = whole_weight(w_out, seqs, owners)
     ends = [sum(CHUNKS[: i + 1]) for i in range(len(CHUNKS))]
     pieces = [
@@ -276,23 +275,16 @@
     weights = (w_query, w_key, w_value, w_beta, beta_gain)
     done = []
     for a in pieces:
-        if done:
-            a, done[-1] = lax.optimization_barrier((a, done[-1]))
         if len(done) == 1:
-            a, w_whole = lax.optimization_barrier((a, w_whole))
-        done.append([chunk_terms(a, *weights, few, g) for g in range(groups)])
-    pairs = [fold([a[g][2] for a in done]) for g in range(groups)]
-    everyone = [lax.all_gather(last, "seq", axis=0) for _, last in pairs]
+            a, done[-1], w_whole = lax.optimization_barrier((a, done[-1], w_whole))
+        done.append(chunk_terms(a, *weights, heads, 0))
+    starts, last = fold([a[2] for a in done])
+    everyone = lax.all_gather(last, "seq", axis=0)
+    where = place.reshape(1).astype(jnp.int32)
+    gain = norm_gain.reshape(1, per)
     rows = []
-    for g in range(groups):
-        normed = emit(
-            place.reshape(1).astype(jnp.int32),
-            everyone[g],
-            pairs[g][0],
-            norm_gain[g * per // groups : (g + 1) * per // groups].reshape(1, -1),
-            [a[g][0] for a in done],
-            [a[g][1] for a in done],
-        )
+    for part, (reads, outs, _) in enumerate(done):
+        normed = emit(part, where, everyone, starts, gain, [reads], [outs])
         rows.append(lax.all_to_all(normed, "head", split_axis=0, concat_axis=0, tiled=True))
     return mix(rows, w_whole)
 

time: 348 us -> 334 us (0.960)
  waiting for transfers between devices: 134 us -> 164 us
  blocking collectives: 53.4 us -> 29 us
  Pallas kernels: 86.3 us -> 72.9 us
  local copies, waits for them, and re-layouts: 27.1 us -> 18.6 us
    all_to_all x1, blocking collectives: 53.4 us -> 29 us  [body(): lax.all_to_all(normed, 'head', split_axis=0, concat_axis=0, tiled=True)]
    all_to_all x0 -> x1, waiting for transfers between devices: none -> 19.7 us  [body(): lax.all_to_all(normed, 'head', split_axis=0, concat_axis=0, tiled=True)]
    ppermute x3, waiting for transfers between devices: 56.5 us -> 68.8 us  [whole_weight(): other = lax.ppermute(held, 'seq', pairs)]
    pallas_call x3 -> x2, Pallas kernels: 63.3 us -> 52.5 us  [chunk_terms(): pl.pallas_call(functools.partial(chunk_kernel, heads), grid=(chunks,), in...]
    unnamed x47 -> x45, local copies, waits for them, and re-layouts: 14.1 us -> 6.77 us
    all_gather x1, waiting for transfers between devices: 39.7 us -> 32.6 us  [body(): everyone = lax.all_gather(last, 'seq', axis=0)]
    all_to_all x0 -> x1, starting transfers between devices: none -> 4.73 us  [body(): lax.all_to_all(normed, 'head', split_axis=0, concat_axis=0, tiled=True)]
    pallas_call x1, Pallas kernels: 6.87 us -> 3.38 us  [fold(): pl.pallas_call(functools.partial(fold_kernel, parts), out_shape=[jax.Shap...]
  transfers between devices with their start and end apart: 10 -> 10, of which waited for: 6 -> 7; matrix products, arithmetic and copies ran while one was open for 9% -> 9% of each run, Pallas kernels for 13% -> 9%
where the time goes in v4:
time: 334 us; the launch traced here: 333 us
  waiting for transfers between devices  164 us (49%)
  Pallas kernels  72.9 us (22%)
  blocking collectives  29 us (9%)
  other arithmetic  20 us (6%)
  local copies, waits for them, and re-layouts  18.6 us (6%)
  starting transfers between devices  14.8 us (4%)
  between operations  13.4 us (4%)
    ppermute x3, waiting for transfers between devices, whole_weight(): other = lax.ppermute(held, 'seq', pairs)  68.8 us
    pallas_call x2, Pallas kernels, chunk_terms(): pl.pallas_call(functools.partial(chunk_kernel, heads), grid=(chunks,), in...  52.5 us
    all_gather x1, waiting for transfers between devices, body(): everyone = lax.all_gather(last, 'seq', axis=0)  32.6 us
    all_to_all x1, blocking collectives, body(): lax.all_to_all(normed, 'head', split_axis=0, concat_axis=0, tiled=True)  29 us
    ppermute x3, waiting for transfers between devices, whole_weight(): turned.append(lax.ppermute(mine, 'head', pairs))  27 us
    all_to_all x1, waiting for transfers between devices, body(): lax.all_to_all(normed, 'head', split_axis=0, concat_axis=0, tiled=True)  19.7 us
    all_gather x2, waiting for transfers between devices, body(): lax.all_gather(tokens[end - size:end], 'head', axis=0)  16.1 us
    another operation x5, other arithmetic, whole_weight(): jnp.stack([jnp.where(upper, other, held), jnp.where(upper, held, other)])  13.5 us
  transfers between devices with their start and end apart: 10, of which 7 were waited for; matrix products, arithmetic and copies ran while one was open for 9% of the time, Pallas kernels for 9%

profile of v4, /device:TPU:0, one launch (start us, length us, event | category | flops | bytes accessed | tf_op | source)
XLA Modules:
  0.0 333.1 jit_solution(16750208050699155835)
XLA Ops:
  6.5 0.0 copy-start
  6.5 0.0 all-gather.9.cloned.1.call-start
  6.5 3.2 fusion
  9.8 0.0 all-gather.9.cloned.1.call-update
  9.8 0.0 all-gather.7.cloned.1.call-start
  9.9 0.0 copy-done
  9.9 3.1 collective-permute-start
  13.0 2.6 collective-permute-start.1
  15.6 1.3 collective-permute-start.2
  16.9 5.3 %collective-permute-done = bf16[64,2048]{1,0:T(8,128)(2,1)S(1)} collective-permute-done((bf16[64,2048]{1,0:T(8,128)(2,1)S(1)}, bf16[64,2048]{1,0:T(8,128)(2,1)S(1)}, u32[]{:S(2)}, u32[]{:S(2)}) %collective-permute-start) | collective-permute-done | bytes 262176 | tf_op jit(solution)/shard_map/ppermute | solution.py:244
  22.3 21.7 %collective-permute-done.1 = bf16[64,2048]{1,0:T(8,128)(2,1)S(1)} collective-permute-done((bf16[64,2048]{1,0:T(8,128)(2,1)S(1)}, bf16[64,2048]{1,0:T(8,128)(2,1)S(1)}, u32[]{:S(2)}, u32[]{:S(2)}) %collective-permute-start.1) | collective-permute-done | bytes 262176 | tf_op jit(solution)/shard_map/ppermute | solution.py:244
  44.0 0.0 collective-permute-done.2
  44.0 0.1 pad_maximum_fusion.2
  44.1 0.1 constant_dynamic-slice_fusion.3
  44.2 0.1 pad_maximum_fusion.3
  44.4 1.5 collective-permute-start.3
  45.9 23.6 %collective-permute-done.3 = bf16[4,64,2048]{2,1,0:T(8,128)(2,1)} collective-permute-done((bf16[4,64,2048]{2,1,0:T(8,128)(2,1)S(1)}, bf16[4,64,2048]{2,1,0:T(8,128)(2,1)}, u32[]{:S(2)}, u32[]{:S(2)}) %collective-permute-start.3) | collective-permute-done | bytes 1048608 | tf_op jit(solution)/shard_map/ppermute | solution.py:257
  69.4 1.4 select_bitcast_fusion.5
  70.8 0.0 copy-start.19
  70.9 1.7 pad_maximum_fusion.1
  72.5 0.0 copy-done.19
  72.5 1.5 collective-permute-start.4
  74.0 0.0 all-gather.7.cloned.1.call-update
  74.0 0.0 all-gather.11.cloned.1.call-start
  74.1 45.3 %collective-permute-done.4 = bf16[2,4,64,2048]{3,2,1,0:T(8,128)(2,1)} collective-permute-done((bf16[2,4,64,2048]{3,2,1,0:T(8,128)(2,1)}, bf16[2,4,64,2048]{3,2,1,0:T(8,128)(2,1)}, u32[]{:S(2)}, u32[]{:S(2)}) %collective-permute-start.4) | collective-permute-done | bytes 2097184 | tf_op jit(solution)/shard_map/ppermute | solution.py:257
  119.3 2.1 select_bitcast_fusion.3
  121.5 0.0 copy-start.20
  121.5 0.0 copy-start.21
  121.5 2.6 pad_maximum_fusion
  124.1 0.0 copy-done.15
  124.2 0.6 copy-done.17
  124.7 0.0 collective-permute-start.5
  124.8 0.3 copy.11
  125.1 0.1 pad.10.wb
  125.2 0.0 all-gather.9.cloned.1.call-done
  125.3 26.3 %chunk_terms.2 = (bf16[4,256,512]{2,1,0:T(8,128)(2,1)S(1)}, f32[4,256,512]{2,1,0:T(8,128)S(1)}, f32[4,4,128,256]{3,2,1,0:T(8,128)S(1)}) custom-call(bf16[4,256,2048]{2,1,0:T(8,128)(2,1)} %bitcast.35, bf16[2048,512]{1,0:T(8,128)(2,1)} %wq.3, bf16[2048,512]{1,0:T(8,128)(2,1)} %wk.3, bf16[2048,512]{1,0:T(8,128)(2,1)} %wv.3, bf16[2048,128]{1,0:T(8,128)(2,1)S(1)} %pad.10.wb, ...), custom_call_target="tpu_custom_call" | custom-call | flops 16106127360 | bytes 14680064 | tf_op jit(solution)/shard_map/chunk_terms/pallas_call | solution.py:93
  151.6 0.0 copy-start.6
  151.6 0.0 collective-permute-done.5
  151.6 0.0 copy-done.16
  151.6 0.0 copy-done.18
  151.6 5.7 %select_bitcast_fusion.1 = (bf16[1,2,2,4,64,2048]{5,4,3,2,1,0:T(8,128)(2,1)S(1)}, bf16[1,2,2,4,64,2048]{5,4,3,2,1,0:T(8,128)(2,1)}) fusion(bf16[2,2,4,64,2048]{4,3,2,1,0:T(8,128)(2,1)} %collective-permute-done.5, pred[]{:T(512)S(6)} %eq.14, bf16[1,2,4,64,2048]{4,3,2,1,0:T(8,128)(2,1)S(1)} %copy-done.18, bf16[1,2,4,64,2048]{4,3,2,1,0:T(8,128)(2,1)S(1)} %copy-done.16), kind=kLoop, calls=%fused_computation.3 | loop fusion | flops 6291456 | bytes 16777216 | tf_op jit(solution)/shard_map/stack | solution.py:259
  157.3 0.0 copy-done.10
  157.3 6.2 %maximum_bitcast_fusion = bf16[4,2,2,2,64,2048]{5,4,0,2,1,3:T(8,128)(2,1)} fusion(bf16[1,2,2,4,64,2048]{5,4,3,2,1,0:T(8,128)(2,1)} %get-tuple-element.32, bf16[1,2,2,4,64,2048]{5,4,3,2,1,0:T(8,128)(2,1)S(1)} %get-tuple-element.31), kind=kLoop, calls=%fused_computation | loop fusion | flops 4194304 | bytes 16777216 | tf_op jit(solution)/shard_map/transpose | solution.py:261
  163.5 8.3 %copy.12 = bf16[4,2,2,2,64,2048]{5,4,3,2,1,0:T(8,128)(2,1)} copy(bf16[4,2,2,2,64,2048]{5,4,0,2,1,3:T(8,128)(2,1)} %maximum_bitcast_fusion) | data formatting | bytes 16777216 | tf_op jit(solution)/shard_map/transpose | solution.py:261
  171.9 16.1 %all-gather.7.cloned.1.call-done = bf16[1024,2048]{1,0:T(8,128)(2,1)} async-done(((bf16[256,2048]{1,0:T(8,128)(2,1)}), bf16[1024,2048]{1,0:T(8,128)(2,1)}) %all-gather.7.cloned.1.call-update) | async-done | bytes 4194320 | tf_op jit(solution)/shard_map/all_gather | solution.py:272
  187.9 1.0 copy-done.13
  189.0 26.2 %chunk_terms.3 = (bf16[4,256,512]{2,1,0:T(8,128)(2,1)S(1)}, f32[4,256,512]{2,1,0:T(8,128)S(1)}, f32[4,4,128,256]{3,2,1,0:T(8,128)S(1)}) custom-call(bf16[4,256,2048]{2,1,0:T(8,128)(2,1)} %bitcast.36, bf16[2048,512]{1,0:T(8,128)(2,1)} %wq.3, bf16[2048,512]{1,0:T(8,128)(2,1)} %wk.3, bf16[2048,512]{1,0:T(8,128)(2,1)} %wv.3, bf16[2048,128]{1,0:T(8,128)(2,1)S(1)} %copy-done.13, ...), custom_call_target="tpu_custom_call" | custom-call | flops 16106127360 | bytes 14680064 | tf_op jit(solution)/shard_map/chunk_terms/pallas_call | solution.py:93
  215.2 0.0 copy-start.14
  215.2 3.4 %fold.1 = (f32[2,4,4,128,256]{4,3,2,1,0:T(8,128)}, bf16[4,128,256]{2,1,0:T(8,128)(2,1)}) custom-call(f32[4,4,128,256]{3,2,1,0:T(8,128)S(1)} %copy-done.7, f32[4,4,128,256]{3,2,1,0:T(8,128)S(1)} %get-tuple-element.23.refs_1_), custom_call_target="tpu_custom_call" | custom-call | tf_op jit(solution)/shard_map/fold/pallas_call | solution.py:142
  218.6 0.0 copy-done.9
  218.6 0.0 all-gather.11.cloned.1.call-update
  218.6 32.6 %all-gather.11.cloned.1.call-done = bf16[32,128,256]{2,1,0:T(8,128)(2,1)} async-done(((bf16[4,128,256]{2,1,0:T(8,128)(2,1)}), bf16[32,128,256]{2,1,0:T(8,128)(2,1)}) %all-gather.11.cloned.1.call-update) | async-done | bytes 2097168 | tf_op jit(solution)/shard_map/all_gather | solution.py:282
  251.3 0.0 copy-done.14
  251.3 1.6 copy-done.2
  252.9 4.4 %emit.3 = bf16[4,256,512]{2,1,0:T(8,128)(2,1)S(1)} custom-call(s32[1]{0:T(128)} %bitcast.place_ref, bf16[8,4,128,256]{3,2,1,0:T(8,128)(2,1)S(1)} %bitcast.27, f32[2,4,4,128,256]{4,3,2,1,0:T(8,128)} %get-tuple-element.25.starts_ref, f32[1,512]{1,0:T(1,128)S(1)} %bitcast.29, bf16[4,256,512]{2,1,0:T(8,128)(2,1)S(1)} %get-tuple-element.28.refs_0_, ...), custom_call_target="tpu_custom_call" | custom-call | tf_op jit(solution)/shard_map/emit/pallas_call | solution.py:188
  257.3 1.0 copy-done.4
  258.3 4.7 %all-to-all-start.1 = ((bf16[4,256,512]{2,1,0:T(8,128)(2,1)}), bf16[4,256,512]{2,1,0:T(8,128)(2,1)S(1)}, u32[]{:S(2)}, u32[]{:S(2)}) async-start(bf16[4,256,512]{2,1,0:T(8,128)(2,1)} %copy-done.4), calls=%async_computation.1 | async-start | bytes 2097152 | tf_op jit(solution)/shard_map/all_to_all | solution.py:288
  263.0 1.2 copy-done.11
  264.2 4.4 %emit.2 = bf16[4,256,512]{2,1,0:T(8,128)(2,1)S(1)} custom-call(s32[1]{0:T(128)} %bitcast.place_ref, bf16[8,4,128,256]{3,2,1,0:T(8,128)(2,1)S(1)} %bitcast.28, f32[2,4,4,128,256]{4,3,2,1,0:T(8,128)} %get-tuple-element.25.starts_ref, f32[1,512]{1,0:T(1,128)S(1)} %bitcast.30, bf16[4,256,512]{2,1,0:T(8,128)(2,1)S(1)} %copy-done.11, f32[4,256,512]{2,1,0:T(8,128)} %copy-done.8), custom_call_target="tpu_custom_call" | custom-call | tf_op jit(solution)/shard_map/emit/pallas_call | solution.py:188
  268.7 0.0 copy-start.5
  268.7 1.0 copy-done.5
  269.7 19.7 %all-to-all-done.1.refs_1_ = bf16[4,256,512]{2,1,0:T(8,128)(2,1)S(1)} async-done(((bf16[4,256,512]{2,1,0:T(8,128)(2,1)}), bf16[4,256,512]{2,1,0:T(8,128)(2,1)S(1)}, u32[]{:S(2)}, u32[]{:S(2)}) %all-to-all-start.1) | async-done | bytes 1048608 | tf_op jit(solution)/shard_map/all_to_all | solution.py:288
  289.3 29.0 %all_to_all.10.refs_0_ = bf16[4,256,512]{2,1,0:T(8,128)(2,1)S(1)} all-to-all(bf16[4,256,512]{2,1,0:T(8,128)(2,1)} %copy-done.5), channel_id=1, replica_groups=mesh['seq'=8,'head'=4] {'head'}, dimensions={0} | all-to-all | bytes 2097152 | tf_op jit(solution)/shard_map/all_to_all | solution.py:288
  318.3 8.2 %mix.1 = bf16[512,2048]{1,0:T(8,128)(2,1)} custom-call(bf16[4,256,512]{2,1,0:T(8,128)(2,1)S(1)} %all_to_all.10.refs_0_, bf16[4,256,512]{2,1,0:T(8,128)(2,1)S(1)} %all-to-all-done.1.refs_1_, bf16[2048,2048]{1,0:T(8,128)(2,1)} %bitcast.31), custom_call_target="tpu_custom_call" | custom-call | tf_op jit(solution)/shard_map/mix/pallas_call | solution.py:224
  (26 shorter events, 0.1 us)
Async XLA Ops:
  6.5 3.3 copy-start
  6.5 118.7 %all-gather.9.cloned.1.call-start = ((), (), s32[]{:S(2)}) async-start(), calls=%async_computation.3 | async-start | bytes 5242880 | tf_op jit(solution)/shard_map/all_gather | solution.py:272
  9.8 178.1 %all-gather.7.cloned.1.call-start = ((), (), s32[]{:S(2)}) async-start(), calls=%async_computation.2 | async-start | bytes 5242880 | tf_op jit(solution)/shard_map/all_gather | solution.py:272
  9.9 12.4 %collective-permute-start = (bf16[64,2048]{1,0:T(8,128)(2,1)S(1)}, bf16[64,2048]{1,0:T(8,128)(2,1)S(1)}, u32[]{:S(2)}, u32[]{:S(2)}) collective-permute-start(bf16[64,2048]{1,0:T(8,128)(2,1)S(1)} %constant_dynamic-slice_fusion.4), channel_id=1, source_target_pairs={{0,1},{1,2},{2,3},{3,0},{4,5},{5,6},{6,7},{7,4},{8,9},{9,10},{10,1... | collective-permute-start | bytes 786440 | tf_op jit(solution)/shard_map/ppermute | solution.py:244
  13.0 31.0 %collective-permute-start.1 = (bf16[64,2048]{1,0:T(8,128)(2,1)S(1)}, bf16[64,2048]{1,0:T(8,128)(2,1)S(1)}, u32[]{:S(2)}, u32[]{:S(2)}) collective-permute-start(bf16[64,2048]{1,0:T(8,128)(2,1)S(1)} %constant_dynamic-slice_fusion.4), channel_id=1, source_target_pairs={{0,2},{1,3},{2,0},{3,1},{4,6},{5,7},{6,4},{7,5},{8,10},{9,11},{10,... | collective-permute-start | bytes 786440 | tf_op jit(solution)/shard_map/ppermute | solution.py:244
  15.6 28.4 %collective-permute-start.2 = (bf16[64,2048]{1,0:T(8,128)(2,1)S(1)}, bf16[64,2048]{1,0:T(8,128)(2,1)S(1)}, u32[]{:S(2)}, u32[]{:S(2)}) collective-permute-start(bf16[64,2048]{1,0:T(8,128)(2,1)S(1)} %constant_dynamic-slice_fusion.4), channel_id=1, source_target_pairs={{0,3},{1,0},{2,1},{3,2},{4,7},{5,4},{6,5},{7,6},{8,11},{9,8},{10,9... | collective-permute-start | bytes 786440 | tf_op jit(solution)/shard_map/ppermute | solution.py:244
  44.4 25.1 %collective-permute-start.3 = (bf16[4,64,2048]{2,1,0:T(8,128)(2,1)S(1)}, bf16[4,64,2048]{2,1,0:T(8,128)(2,1)}, u32[]{:S(2)}, u32[]{:S(2)}) collective-permute-start(bf16[4,64,2048]{2,1,0:T(8,128)(2,1)S(1)} %pad_maximum_fusion.3), channel_id=1, source_target_pairs={{0,8},{4,12},{8,0},{12,4},{16,24},{20,28},{24,16},{28,20},{1,9},{5... | collective-permute-start | bytes 3145736 | tf_op jit(solution)/shard_map/ppermute | solution.py:257
  70.8 1.7 copy-start.19
  72.5 46.8 %collective-permute-start.4 = (bf16[2,4,64,2048]{3,2,1,0:T(8,128)(2,1)}, bf16[2,4,64,2048]{3,2,1,0:T(8,128)(2,1)}, u32[]{:S(2)}, u32[]{:S(2)}) collective-permute-start(bf16[2,4,64,2048]{3,2,1,0:T(8,128)(2,1)} %pad_maximum_fusion.1), channel_id=1, source_target_pairs={{0,16},{4,20},{8,24},{12,28},{16,0},{20,4},{24,8},{28,12},{1,17},{... | collective-permute-start | bytes 6291464 | tf_op jit(solution)/shard_map/ppermute | solution.py:257
  74.0 177.3 %all-gather.11.cloned.1.call-start = ((), (), s32[]{:S(2)}) async-start(), calls=%async_computation.4 | async-start | bytes 2359296 | tf_op jit(solution)/shard_map/all_gather | solution.py:282
  121.5 2.7 copy-start.15
  121.5 3.3 copy-start.17
  121.5 3.3 copy-start.20
  121.5 3.7 %copy-start.21 = (f32[4]{0:T(128)S(1)}, f32[4]{0:T(128)}, u32[]{:S(2)}) copy-start(f32[4]{0:T(128)} %param.13) | copy-start | bytes 52
  124.7 26.9 %collective-permute-start.5 = (bf16[2,2,4,64,2048]{4,3,2,1,0:T(8,128)(2,1)}, bf16[2,2,4,64,2048]{4,3,2,1,0:T(8,128)(2,1)}, u32[]{:S(2)}, u32[]{:S(2)}) collective-permute-start(bf16[2,2,4,64,2048]{4,3,2,1,0:T(8,128)(2,1)} %pad_maximum_fusion), channel_id=1, source_target_pairs={{0,4},{4,0},{8,12},{12,8},{16,20},{20,16},{24,28},{28,24},{1,5},{5... | collective-permute-start | bytes 12582920 | tf_op jit(solution)/shard_map/ppermute | solution.py:257
  125.2 26.4 %copy-start.12 = (bf16[2048,128]{1,0:T(8,128)(2,1)}, bf16[2048,128]{1,0:T(8,128)(2,1)S(1)}, u32[]{:S(2)}) copy-start(bf16[2048,128]{1,0:T(8,128)(2,1)S(1)} %pad.10.wb) | copy-start | bytes 1572868
  125.2 26.4 %copy-start.16 = (bf16[1,2,4,64,2048]{4,3,2,1,0:T(8,128)(2,1)S(1)}, bf16[1,2,4,64,2048]{4,3,2,1,0:T(8,128)(2,1)}, u32[]{:S(2)}) copy-start(bf16[1,2,4,64,2048]{4,3,2,1,0:T(8,128)(2,1)} %copy-done.15) | copy-start | bytes 6291460
  125.3 26.4 %copy-start.18 = (bf16[1,2,4,64,2048]{4,3,2,1,0:T(8,128)(2,1)S(1)}, bf16[1,2,4,64,2048]{4,3,2,1,0:T(8,128)(2,1)}, u32[]{:S(2)}) copy-start(bf16[1,2,4,64,2048]{4,3,2,1,0:T(8,128)(2,1)} %copy-done.17) | copy-start | bytes 6291460
  151.6 5.7 %copy-start.6 = (f32[4,4,128,256]{3,2,1,0:T(8,128)}, f32[4,4,128,256]{3,2,1,0:T(8,128)S(1)}, u32[]{:S(2)}) copy-start(f32[4,4,128,256]{3,2,1,0:T(8,128)S(1)} %get-tuple-element.21.refs_0_) | copy-start | bytes 6291460
  151.6 5.7 %copy-start.8 = (f32[4,256,512]{2,1,0:T(8,128)}, f32[4,256,512]{2,1,0:T(8,128)S(1)}, u32[]{:S(2)}) copy-start(f32[4,256,512]{2,1,0:T(8,128)S(1)} %get-tuple-element.27.refs_1_) | copy-start | bytes 6291460
  151.6 5.7 %copy-start.10 = (bf16[4,256,512]{2,1,0:T(8,128)(2,1)}, bf16[4,256,512]{2,1,0:T(8,128)(2,1)S(1)}, u32[]{:S(2)}) copy-start(bf16[4,256,512]{2,1,0:T(8,128)(2,1)S(1)} %get-tuple-element.26.refs_0_) | copy-start | bytes 3145732
  187.9 1.0 copy-start.13
  189.0 26.2 %copy-start.7 = (f32[4,4,128,256]{3,2,1,0:T(8,128)S(1)}, f32[4,4,128,256]{3,2,1,0:T(8,128)}, u32[]{:S(2)}) copy-start(f32[4,4,128,256]{3,2,1,0:T(8,128)} %copy-done.6) | copy-start | bytes 6291460
  215.2 3.4 %copy-start.9 = (f32[4,256,512]{2,1,0:T(8,128)}, f32[4,256,512]{2,1,0:T(8,128)S(1)}, u32[]{:S(2)}) copy-start(f32[4,256,512]{2,1,0:T(8,128)S(1)} %get-tuple-element.29.refs_1_) | copy-start | bytes 6291460
  215.2 36.1 %copy-start.14 = (f32[512]{0:T(512)S(1)}, f32[512]{0:T(512)}, u32[]{:S(2)}) copy-start(f32[512]{0:T(512)} %param.14) | copy-start | bytes 6148
  251.3 1.6 copy-start.2
  257.3 1.0 copy-start.4
  258.3 4.7 %copy-start.3 = (bf16[32,128,256]{2,1,0:T(8,128)(2,1)S(1)}, bf16[32,128,256]{2,1,0:T(8,128)(2,1)}, u32[]{:S(2)}) copy-start(bf16[32,128,256]{2,1,0:T(8,128)(2,1)} %all-gather.11.cloned.1.call-done) | copy-start | bytes 6291460
  258.3 31.1 %all-to-all-start.1 = ((bf16[4,256,512]{2,1,0:T(8,128)(2,1)}), bf16[4,256,512]{2,1,0:T(8,128)(2,1)S(1)}, u32[]{:S(2)}, u32[]{:S(2)}) async-start(bf16[4,256,512]{2,1,0:T(8,128)(2,1)} %copy-done.4), calls=%async_computation.1 | async-start | bytes 2097152 | tf_op jit(solution)/shard_map/all_to_all | solution.py:288
  263.0 1.2 copy-start.11
  268.7 1.0 copy-start.5
  318.3 8.2 %copy-start.1 = (bf16[512,2048]{1,0:T(8,128)(2,1)S(1)}, bf16[512,2048]{1,0:T(8,128)(2,1)}, u32[]{:S(2)}) copy-start(bf16[512,2048]{1,0:T(8,128)(2,1)} %param.15) | copy-start | bytes 6291460
Sparse Core Ops, SparseCore 0:
  9.9 96.1 all-gather.8
  107.7 80.1 all-gather.6
  218.8 32.4 all-gather.10
